TPU v7x, 32 devices: a whole 2x2x4 slice. The times are simulated.
32 devices in a mesh: dp: 16 (over z, y, core), tensor: 2 (over x).
Axes of the slice: x: 2, y: 2, z: 4, core: 2. Of those that a mesh axis runs over, the one named last changes fastest.
Arguments:
- tokens: bfloat16 [16, 1024, 768], P('dp', 'tensor'), may hold values from -6 to 6
- cotangent: bfloat16 [16, 1024, 768], P('dp', 'tensor'), may hold values from -6 to 6
- norm_in: float32 [768], replicated, may hold values from 0.5 to 1.5
- gate_inner_projection: bfloat16 [768, 2, 1536], P('dp', None, 'tensor'), may hold values from -0.21875 to 0.21875
- proj_bc: bfloat16 [768, 256], P('dp'), may hold values from -0.21875 to 0.21875
- proj_dt: bfloat16 [768, 24], P('dp', 'tensor'), may hold values from -0.21875 to 0.21875
- conv_inner: float32 [4, 1536], P(None, 'tensor'), may hold values from -3 to 3
- bias_inner: float32 [1536], P('tensor'), may hold values from -0.5 to 0.5
- conv_bc: float32 [4, 256], replicated, may hold values from -3 to 3
- bias_bc: float32 [256], replicated, may hold values from -0.5 to 0.5
- step_bias: float32 [24], P('tensor'), may hold values from -7 to -2
- log_decay: float32 [24], P('tensor'), may hold values from -1.5 to 2.5
- skip_gain: float32 [24], P('tensor'), may hold values from 0.5 to 2
- norm_gate: float32 [1536], P('tensor'), may hold values from 0.5 to 1.5
- proj_out: bfloat16 [1536, 768], P('tensor', 'dp'), may hold values from -0.15625 to 0.15625
Outputs:
- block_out: bfloat16 [16, 1024, 768], P('dp', 'tensor')
- input_grad: float32 [16, 1024, 768], P('dp', 'tensor')
- grad_norm_in: float32 [768], replicated
- grad_proj_zx: float32 [768, 2, 1536], P('dp', None, 'tensor')
- grad_proj_bc: float32 [768, 256], P('dp')
- grad_proj_dt: float32 [768, 24], P('dp', 'tensor')
- grad_conv_inner: float32 [4, 1536], P(None, 'tensor')
- grad_bias_inner: float32 [1536], P('tensor')
- grad_conv_bc: float32 [4, 256], replicated
- grad_bias_bc: float32 [256], replicated
- grad_step_bias: float32 [24], P('tensor')
- grad_log_decay: float32 [24], P('tensor')
- grad_skip_gain: float32 [24], P('tensor')
- grad_norm_gate: float32 [1536], P('tensor')
- grad_proj_out: float32 [1536, 768], P('tensor', 'dp')
All inputs are finite; a program needn't handle non-finite values.
Results may differ from a plain program's by a relative error of at most 0.018.
Values may be sent and summed in bfloat16 or wider, within the bound.
A program may use at most 128 MiB of HBM per device.

v0:
```python
import jax
import jax.numpy as jnp
from jax import lax
from jax.sharding import PartitionSpec as P

NSTATE = 128
SPAN = 256
INNER = 1536


EPSILON = 1e-05
NEARLY = lax.Precision.HIGH


def rounded(values):
    return lax.optimization_barrier(values.astype(jnp.bfloat16)).astype(jnp.float32)


def contract(left, right, left_dim, right_dim):
    return lax.dot_general(
        left, right, (((left_dim,), (right_dim,)), ((), ())), preferred_element_type=jnp.float32
    )


def scan_block(carry_state, block_data):
    scaled_in, key_matrix, query_matrix, decay_factor = block_data
    size_q = decay_factor.shape[0]
    cumulative = jnp.cumsum(decay_factor, axis=0)
    row_index = lax.broadcasted_iota(jnp.int32, (size_q, size_q), 0)
    col_index = lax.broadcasted_iota(jnp.int32, (size_q, size_q), 1)
    causal = (col_index <= row_index)[None]
    log_gap = cumulative.T[:, :, None] - cumulative.T[:, None, :]
    decay_table = jnp.exp(jnp.where(causal, log_gap, -jnp.inf))
    scores = jnp.dot(
        query_matrix.astype(jnp.bfloat16),
        key_matrix.astype(jnp.bfloat16).T,
        preferred_element_type=jnp.float32,
    )
    weights = decay_table * scores[None]
    intra_out = jnp.einsum("hij,jhp->ihp", weights, scaled_in, precision=NEARLY)
    inter_out = (
        jnp.einsum("in,hpn->ihp", query_matrix, carry_state, precision=NEARLY)
        * jnp.exp(cumulative)[:, :, None]
    )
    tail_decay = jnp.exp(cumulative[-1][None, :] - cumulative)
    fresh_state = jnp.einsum(
        "jhp,jn->hpn", scaled_in * tail_decay[:, :, None], key_matrix, precision=NEARLY
    )
    carry_state = jnp.exp(cumulative[-1])[:, None, None] * carry_state + fresh_state
    return (carry_state, intra_out + inter_out)


def scan_heads(scaled_in, key_matrix, query_matrix, decay_factor):
    length, head_count, head_width = scaled_in.shape
    block_count = length // SPAN
    blocks = (
        scaled_in.reshape(block_count, SPAN, head_count, head_width),
        key_matrix.reshape(block_count, SPAN, key_matrix.shape[1]),
        query_matrix.reshape(block_count, SPAN, query_matrix.shape[1]),
        decay_factor.reshape(block_count, SPAN, head_count),
    )
    start_state = jnp.zeros((head_count, head_width, key_matrix.shape[1]), jnp.float32)
    final_state, outputs = lax.scan(jax.checkpoint(scan_block), start_state, blocks)
    return outputs.reshape(length, head_count, head_width)


def causal_conv(values, kernel, offset):
    tap_count = kernel.shape[0]
    length = values.shape[0]
    padded_tokens = jnp.pad(values, ((tap_count - 1, 0), (0, 0)))
    summed = jnp.zeros_like(values) + offset[None, :]
    for position in range(tap_count):
        summed = summed + kernel[position][None, :] * padded_tokens[position : position + length]
    return summed


def mixer(inner_act, state_mats, step_raw, step_bias, log_decay, skip_gain):
    length = inner_act.shape[0]
    head_count = step_raw.shape[1]
    step_size = jax.nn.softplus(step_raw + step_bias)
    decay_factor = -jnp.exp(log_decay) * step_size
    per_head = inner_act.reshape(length, head_count, -1)
    scaled_in = per_head * step_size[:, :, None]
    scanned = scan_heads(scaled_in, state_mats[:, :NSTATE], state_mats[:, NSTATE:], decay_factor)
    return (scanned + skip_gain[None, :, None] * per_head).reshape(length, -1)


def pre_norm(values, gain):
    inv_rms = lax.rsqrt(jnp.mean(values * values, axis=-1, keepdims=True) + EPSILON)
    return values * inv_rms * gain


def conv_part(inner_raw, state_raw, conv_inner, bias_inner, conv_bc, bias_bc):
    return (
        jax.nn.silu(causal_conv(inner_raw, conv_inner, bias_inner)),
        jax.nn.silu(causal_conv(state_raw, conv_bc, bias_bc)),
    )


def gating(scanned, gate_z):
    return scanned * jax.nn.silu(gate_z)


def on_device(
    tokens,
    cotangent,
    norm_in,
    gate_inner_projection,
    proj_bc,
    proj_dt,
    conv_inner,
    bias_inner,
    conv_bc,
    bias_bc,
    step_bias,
    log_decay,
    skip_gain,
    norm_gate,
    proj_out,
):
    token_rows = tokens[0].astype(jnp.float32)
    norm_value, norm_pull = jax.vjp(pre_norm, token_rows, norm_in)
    normalized_rows = norm_value.astype(jnp.bfloat16)
    gathered = lax.all_gather(normalized_rows, "tensor", axis=0, tiled=True)
    full_zx, full_dt, full_bc, full_out = (
        lax.all_gather(gate_inner_projection, "dp", axis=0, tiled=True),
        lax.all_gather(proj_dt, "dp", axis=0, tiled=True),
        lax.all_gather(proj_bc, "dp", axis=0, tiled=True),
        lax.all_gather(proj_out, "dp", axis=1, tiled=True),
    )
    inner_width = gate_inner_projection.shape[2]
    model_width = full_zx.shape[0]
    flat_zx = full_zx.reshape(model_width, 2 * inner_width)
    inner_gate_values = jnp.dot(gathered, flat_zx, preferred_element_type=jnp.float32)
    state_raw = jnp.dot(gathered, full_bc, preferred_element_type=jnp.float32)
    step_raw = jnp.dot(gathered, full_dt, preferred_element_type=jnp.float32)
    gate_z = inner_gate_values[:, :inner_width]
    inner_raw = inner_gate_values[:, inner_width:]
    conv_values, conv_pull = jax.vjp(
        conv_part, inner_raw, state_raw, conv_inner, bias_inner, conv_bc, bias_bc
    )
    inner_act = rounded(conv_values[0])
    state_mats = rounded(conv_values[1])
    scanned, mix_pull = jax.vjp(
        mixer, inner_act, state_mats, step_raw, step_bias, log_decay, skip_gain
    )
    gated, gate_pull = jax.vjp(gating, scanned, gate_z)
    squares = lax.psum(jnp.sum(gated * gated, axis=1), "tensor")
    gate_scale = lax.rsqrt(squares / INNER + EPSILON)[:, None]
    gate_normed = (gated * gate_scale * norm_gate).astype(jnp.bfloat16)
    branch = lax.psum_scatter(
        jnp.dot(gate_normed, full_out, preferred_element_type=jnp.float32).astype(jnp.bfloat16),
        "tensor",
        scatter_dimension=0,
        tiled=True,
    ).astype(jnp.float32)
    block_out = (token_rows + branch).astype(jnp.bfloat16)[None]
    cot_whole = lax.all_gather(cotangent[0], "tensor", axis=0, tiled=True)
    d_normed_gate = contract(cot_whole, full_out, 1, 1)
    grad_out = contract(gate_normed, cot_whole, 0, 0)
    weighted = d_normed_gate * norm_gate
    cross = lax.psum(jnp.sum(weighted * gated, axis=1), "tensor")[:, None]
    d_gated = gate_scale * weighted - gated * (gate_scale * gate_scale * gate_scale) * cross / INNER
    grad_norm_gate = jnp.sum(d_normed_gate * gated * gate_scale, axis=0)
    d_scanned, d_gate_z = gate_pull(d_gated)
    d_inner_act, d_state_mats, d_step_full, grad_step_bias, grad_log_decay, grad_skip_gain = (
        mix_pull(d_scanned)
    )
    d_inner_raw, d_state_raw, grad_conv_inner, grad_bias_inner, grad_conv_bc, grad_bias_bc = (
        conv_pull((d_inner_act, d_state_mats))
    )
    d_gate_inner = jnp.concatenate([d_gate_z, d_inner_raw], axis=1).astype(jnp.bfloat16)
    d_step_low = d_step_full.astype(jnp.bfloat16)
    d_partial = contract(d_gate_inner, flat_zx, 1, 1) + contract(d_step_low, full_dt, 1, 1)
    d_rows, d_state_rows = (
        lax.psum_scatter(
            d_partial.astype(jnp.bfloat16), "tensor", scatter_dimension=0, tiled=True
        ).astype(jnp.float32),
        lax.psum_scatter(
            d_state_raw.astype(jnp.bfloat16), "tensor", scatter_dimension=0, tiled=True
        ).astype(jnp.float32),
    )
    d_state_low = d_state_rows.astype(jnp.bfloat16)
    d_rows = d_rows + contract(d_state_low, full_bc, 1, 1)
    d_tokens, grad_norm_in = norm_pull(d_rows)
    input_grad = (cotangent[0].astype(jnp.float32) + d_tokens)[None]
    grad_zx = contract(gathered, d_gate_inner, 0, 0).reshape(model_width, 2, inner_width)
    grad_dt = contract(gathered, d_step_low, 0, 0)
    grad_bc = contract(normalized_rows, d_state_low, 0, 0)
    grad_zx, grad_dt, grad_bc, grad_out = (
        lax.psum_scatter(
            grad_zx.astype(jnp.bfloat16), "dp", scatter_dimension=0, tiled=True
        ).astype(jnp.float32),
        lax.psum_scatter(
            grad_dt.astype(jnp.bfloat16), "dp", scatter_dimension=0, tiled=True
        ).astype(jnp.float32),
        lax.psum_scatter(
            grad_bc.astype(jnp.bfloat16), "dp", scatter_dimension=0, tiled=True
        ).astype(jnp.float32),
        lax.psum_scatter(
            grad_out.astype(jnp.bfloat16), "dp", scatter_dimension=1, tiled=True
        ).astype(jnp.float32),
    )
    (
        grad_conv_inner,
        grad_bias_inner,
        grad_step_bias,
        grad_log_decay,
        grad_skip_gain,
        grad_norm_gate,
        grad_norm_in,
        grad_conv_bc,
        grad_bias_bc,
    ) = lax.psum(
        (
            grad_conv_inner,
            grad_bias_inner,
            grad_step_bias,
            grad_log_decay,
            grad_skip_gain,
            grad_norm_gate,
            grad_norm_in,
            grad_conv_bc,
            grad_bias_bc,
        ),
        "dp",
    )
    grad_bc, grad_norm_in, grad_conv_bc, grad_bias_bc = (
        lax.psum(grad_bc.astype(jnp.bfloat16), "tensor").astype(jnp.float32),
        lax.psum(grad_norm_in.astype(jnp.bfloat16), "tensor").astype(jnp.float32),
        lax.psum(grad_conv_bc.astype(jnp.bfloat16), "tensor").astype(jnp.float32),
        lax.psum(grad_bias_bc.astype(jnp.bfloat16), "tensor").astype(jnp.float32),
    )
    return (
        block_out,
        input_grad,
        grad_norm_in,
        grad_zx,
        grad_bc,
        grad_dt,
        grad_conv_inner,
        grad_bias_inner,
        grad_conv_bc,
        grad_bias_bc,
        grad_step_bias,
        grad_log_decay,
        grad_skip_gain,
        grad_norm_gate,
        grad_out,
    )


def solution(mesh):
    placed = (
        P("dp", "tensor", None),
        P("dp", "tensor", None),
        P(),
        P("dp", None, "tensor"),
        P("dp", None),
        P("dp", "tensor"),
        P(None, "tensor"),
        P("tensor"),
        P(),
        P(),
        P("tensor"),
        P("tensor"),
        P("tensor"),
        P("tensor"),
        P("tensor", "dp"),
    )
    return jax.shard_map(
        on_device,
        mesh=mesh,
        in_specs=placed,
        out_specs=(
            P("dp", "tensor", None),
            P("dp", "tensor", None),
            P(),
            P("dp", None, "tensor"),
            P("dp", None),
            P("dp", "tensor"),
            P(None, "tensor"),
            P("tensor"),
            P(),
            P(),
            P("tensor"),
            P("tensor"),
            P("tensor"),
            P("tensor"),
            P("tensor", "dp"),
        ),
        check_vma=False,
    )
```

profile of v0, /device:TPU:0, one launch (start us, length us, event | category | flops | bytes accessed | tf_op | source)
XLA Modules:
  0.0 802.9 jit_solution(5526248737848147252)
XLA Ops:
  15.8 23.2 %all-gather.1 = bf16[16,48,12]{1,2,0:T(8,128)(2,1)S(1)} all-gather(bf16[1,48,12]{1,2,0:T(8,128)(2,1)S(1)} %bitcast.360), channel_id=1, replica_groups=mesh['dp'=16,'tensor'=2] {'dp'}, dimensions={0}, use_global_device_ids=true | all-gather | bytes 19584 | tf_op jit(solution)/shard_map/all_gather | solution.py:127
  39.2 18.6 %all_gather.21 = bf16[768,256]{1,0:T(8,128)(2,1)S(1)} all-gather(bf16[48,256]{1,0:T(8,128)(2,1)S(1)} %copy-done.31), channel_id=1, replica_groups=mesh['dp'=16,'tensor'=2] {'dp'}, dimensions={0}, use_global_device_ids=true | all-gather | bytes 417792 | tf_op jit(solution)/shard_map/all_gather | solution.py:128
  70.5 16.3 %all-gather.9.cloned.1.call-done = bf16[768,2,768]{2,1,0:T(2,128)(2,1)} async-done(((bf16[48,2,768]{2,1,0:T(2,128)(2,1)}), bf16[768,2,768]{2,1,0:T(2,128)(2,1)}) %all-gather.9.cloned.1.call-update) | async-done | bytes 2359312 | tf_op jit(solution)/shard_map/all_gather | solution.py:126
  111.2 112.4 %while.39 = (s32[]{:T(128)}, f32[12,64,128]{2,1,0:T(8,128)S(1)}, f32[4,256,12,64]{1,0,3,2:T(4,128)}, f32[4,12,64,128]{3,2,1,0:T(8,128)}, f32[4,256,12]{1,2,0:T(8...) while((s32[]{:T(128)}, f32[12,64,128]{2,1,0:T(8,128)S(1)}, ...), condition=%wide.region_4.5_spmd.clone, body=%wide.region_1.4_spmd.clone.sunk | while | flops 624593920 | bytes 10333848 | solution.py:63
  121.5 17.9 %dynamic_update_slice.66 = f32[4,256,12,64]{1,0,3,2:T(4,128)} dynamic-update-slice(f32[4,256,12,64]{1,0,3,2:T(4,128)} %get-tuple-element.842, f32[1,256,12,64]{1,0,3,2:T(1,128)S(1)} %copy.217, s32[]{:T(128)S(6)} %copy.239, s32[]{:T(128)} %constant.129.clone.1..sunk, s32[]{:T(128)} %constant.129.clone.1..sunk, s32[]{:T(128)} %constant.129.clone.1..sunk) | dynamic-update-slice | bytes 1572868 | tf_op jit(solution)/shard_map/jvp()/while/body/jit(dynamic_update_index_in_dim)/dynamic_update_slice | solution.py:63
  149.6 17.9 %dynamic_update_slice.66 = f32[4,256,12,64]{1,0,3,2:T(4,128)} dynamic-update-slice(f32[4,256,12,64]{1,0,3,2:T(4,128)} %get-tuple-element.842, f32[1,256,12,64]{1,0,3,2:T(1,128)S(1)} %copy.217, s32[]{:T(128)S(6)} %copy.239, s32[]{:T(128)} %constant.129.clone.1..sunk, s32[]{:T(128)} %constant.129.clone.1..sunk, s32[]{:T(128)} %constant.129.clone.1..sunk) | dynamic-update-slice | bytes 1572868 | tf_op jit(solution)/shard_map/jvp()/while/body/jit(dynamic_update_index_in_dim)/dynamic_update_slice | solution.py:63
  177.7 17.9 %dynamic_update_slice.66 = f32[4,256,12,64]{1,0,3,2:T(4,128)} dynamic-update-slice(f32[4,256,12,64]{1,0,3,2:T(4,128)} %get-tuple-element.842, f32[1,256,12,64]{1,0,3,2:T(1,128)S(1)} %copy.217, s32[]{:T(128)S(6)} %copy.239, s32[]{:T(128)} %constant.129.clone.1..sunk, s32[]{:T(128)} %constant.129.clone.1..sunk, s32[]{:T(128)} %constant.129.clone.1..sunk) | dynamic-update-slice | bytes 1572868 | tf_op jit(solution)/shard_map/jvp()/while/body/jit(dynamic_update_index_in_dim)/dynamic_update_slice | solution.py:63
  205.8 17.9 %dynamic_update_slice.66 = f32[4,256,12,64]{1,0,3,2:T(4,128)} dynamic-update-slice(f32[4,256,12,64]{1,0,3,2:T(4,128)} %get-tuple-element.842, f32[1,256,12,64]{1,0,3,2:T(1,128)S(1)} %copy.217, s32[]{:T(128)S(6)} %copy.239, s32[]{:T(128)} %constant.129.clone.1..sunk, s32[]{:T(128)} %constant.129.clone.1..sunk, s32[]{:T(128)} %constant.129.clone.1..sunk) | dynamic-update-slice | bytes 1572868 | tf_op jit(solution)/shard_map/jvp()/while/body/jit(dynamic_update_index_in_dim)/dynamic_update_slice | solution.py:63
  223.7 4.3 copy.195
  230.8 5.1 multiply_reduce_fusion.12
  236.0 4.9 psum.105
  240.9 6.6 multiply_reduce_fusion.4
  247.5 4.9 psum.106
  252.4 7.8 multiply_reduce_fusion.5
  269.5 156.4 %while.40 = (s32[]{:T(128)}, f32[12,64,128]{2,1,0:T(8,128)S(1)}, f32[4,256,12,64]{1,0,3,2:T(4,128)}, f32[4,256,128]{2,1,0:T(8,128)}, f32[4,256,128]{2,1,0:T(8,12...) while((s32[]{:T(128)}, f32[12,64,128]{2,1,0:T(8,128)S(1)}, ...), condition=%wide.region_22.23_spmd.clone, body=%wide.region_10.22_spmd.clone.sunk | while | flops 1422057472 | bytes 25541008 | solution.py:63
  290.7 17.9 %dynamic_update_slice.69 = f32[4,256,12,64]{1,0,3,2:T(4,128)} dynamic-update-slice(f32[4,256,12,64]{1,0,3,2:T(4,128)} %get-tuple-element.882, f32[1,256,12,64]{1,0,3,2:T(1,128)S(1)} %copy.224, s32[]{:T(128)S(6)} %sub.264, s32[]{:T(128)} %constant.129.clone.1..sunk.1, s32[]{:T(128)} %constant.129.clone.1..sunk.1, s32[]{:T(128)} %constant.129.clone.1..sunk.1) | dynamic-update-slice | bytes 1572868 | tf_op jit(solution)/shard_map/transpose(jvp())/while/body/jit(dynamic_update_index_in_dim)/dynamic_update_slice | solution.py:63
  329.8 17.9 %dynamic_update_slice.69 = f32[4,256,12,64]{1,0,3,2:T(4,128)} dynamic-update-slice(f32[4,256,12,64]{1,0,3,2:T(4,128)} %get-tuple-element.882, f32[1,256,12,64]{1,0,3,2:T(1,128)S(1)} %copy.224, s32[]{:T(128)S(6)} %sub.264, s32[]{:T(128)} %constant.129.clone.1..sunk.1, s32[]{:T(128)} %constant.129.clone.1..sunk.1, s32[]{:T(128)} %constant.129.clone.1..sunk.1) | dynamic-update-slice | bytes 1572868 | tf_op jit(solution)/shard_map/transpose(jvp())/while/body/jit(dynamic_update_index_in_dim)/dynamic_update_slice | solution.py:63
  368.9 17.9 %dynamic_update_slice.69 = f32[4,256,12,64]{1,0,3,2:T(4,128)} dynamic-update-slice(f32[4,256,12,64]{1,0,3,2:T(4,128)} %get-tuple-element.882, f32[1,256,12,64]{1,0,3,2:T(1,128)S(1)} %copy.224, s32[]{:T(128)S(6)} %sub.264, s32[]{:T(128)} %constant.129.clone.1..sunk.1, s32[]{:T(128)} %constant.129.clone.1..sunk.1, s32[]{:T(128)} %constant.129.clone.1..sunk.1) | dynamic-update-slice | bytes 1572868 | tf_op jit(solution)/shard_map/transpose(jvp())/while/body/jit(dynamic_update_index_in_dim)/dynamic_update_slice | solution.py:63
  408.0 17.9 %dynamic_update_slice.69 = f32[4,256,12,64]{1,0,3,2:T(4,128)} dynamic-update-slice(f32[4,256,12,64]{1,0,3,2:T(4,128)} %get-tuple-element.882, f32[1,256,12,64]{1,0,3,2:T(1,128)S(1)} %copy.224, s32[]{:T(128)S(6)} %sub.264, s32[]{:T(128)} %constant.129.clone.1..sunk.1, s32[]{:T(128)} %constant.129.clone.1..sunk.1, s32[]{:T(128)} %constant.129.clone.1..sunk.1) | dynamic-update-slice | bytes 1572868 | tf_op jit(solution)/shard_map/transpose(jvp())/while/body/jit(dynamic_update_index_in_dim)/dynamic_update_slice | solution.py:63
  425.9 5.4 reshape.408
  445.3 8.1 %multiply_reduce_fusion.8 = (f32[768]{0:T(1024)}, f32[768]{0:T(1024)}, f32[768]{0:T(1024)}, f32[768]{0:T(1024)}, f32[768]{0:T(1024)}, /*index=5*/f32[1024,768]{1,0:T(8,128)}) fusion(f32[1024,768]{1,0:T(8,128)S(1)} %copy-done.4, f32[1024,1536]{1,0:T(8,128)} %copy-done.6, f32[1024,768]{1,0:T(8,128)} %get-tuple-element.611, f32[1024,768]{1,0:T(8,128)} %copy.136, ...), kind=kLoop, calls=%fused_computation.141 | loop fusion | flops 16511232 | bytes 22038528 | tf_op jit(solution)/shard_map/transpose(jvp())/reduce_sum | solution.py:73
  455.3 6.7 broadcast_multiply_fusion.1
  462.0 5.7 fusion.97
  473.0 6.1 convert_element_type.189
  483.3 5.2 fusion.99
  504.2 10.6 %reduce-scatter.19.cloned.1.call-done = bf16[48,12]{1,0:T(8,128)(2,1)} async-done(((bf16[768,12]{1,0:T(8,128)(2,1)}), bf16[48,12]{1,0:T(8,128)(2,1)}) %reduce-scatter.19.cloned.1.call-update) | async-done | bytes 1168
  516.2 100.7 %all-reduce.27.cloned.1.call-done = bf16[768,2,768]{2,1,0:T(2,128)(2,1)} async-done(((bf16[768,2,768]{2,1,0:T(2,128)(2,1)}), bf16[768,2,768]{2,1,0:T(2,128)(2,1)}) %all-reduce.27.cloned.1.call-update) | async-done | bytes 2359312
  618.6 59.7 %reduce-scatter.17.cloned.1.call-done = bf16[768,48]{0,1:T(8,128)(2,1)} async-done(((bf16[768,768]{0,1:T(8,128)(2,1)}), bf16[768,48]{0,1:T(8,128)(2,1)}) %reduce-scatter.17.cloned.1.call-update) | async-done | bytes 73744 | tf_op jit(solution)/shard_map/reduce_scatter | solution.py:200
  679.9 26.5 %reduce-scatter.11.cloned.1.call-done = bf16[512,768]{1,0:T(8,128)(2,1)} async-done(((bf16[1024,768]{1,0:T(8,128)(2,1)}), bf16[512,768]{1,0:T(8,128)(2,1)}) %reduce-scatter.11.cloned.1.call-update) | async-done | bytes 786448 | tf_op jit(solution)/shard_map/reduce_scatter | solution.py:176
  709.2 61.8 %all-reduce.23 = (bf16[768]{0:T(1024)(128)(2,1)S(1)}, f32[4,768]{1,0:T(4,128)}, f32[768]{0:T(1024)}, bf16[4,256]{1,0:T(4,128)(2,1)S(1)}, bf16[256]{0:T(256)(128)...) all-reduce(f32[768]{0:T(1024)} %get-tuple-element.532, ...), channel_id=1, replica_groups=mesh['dp'=16,'tensor'=2] {'dp'}, use_global_device_ids=true, to_apply=%region_28.29 | all-reduce | flops 6692 | bytes 49440 | tf_op jit(solution)/shard_map/psum | solution.py:214
  770.9 8.7 %all-reduce.24 = (bf16[768]{0:T(1024)(128)(2,1)S(1)}, bf16[48,256]{1,0:T(8,128)(2,1)S(1)}, bf16[4,256]{1,0:T(4,128)(2,1)S(1)}, bf16[256]{0:T(256)(128)(2,1)S(1)}) all-reduce(bf16[768]{0:T(1024)(128)(2,1)S(1)} %get-tuple-element.585, ...), channel_id=1, replica_groups=mesh['dp'=16,'tensor'=2] {'tensor'}, use_global_device_ids=true, to_apply=%region_29.30 | all-reduce | flops 14336 | bytes 57344 | tf_op jit(solution)/shard_map/psum | solution.py:230
  782.7 10.3 %reduce-scatter.9.cloned.1.call-done = bf16[512,768]{1,0:T(8,128)(2,1)} async-done(((bf16[1024,768]{1,0:T(8,128)(2,1)}), bf16[512,768]{1,0:T(8,128)(2,1)}) %reduce-scatter.9.cloned.1.call-update) | async-done | bytes 786448 | tf_op jit(solution)/shard_map/reduce_scatter | solution.py:151
  (488 shorter events, 236.4 us)
Async XLA Ops:
  7.2 8.5 %copy-start.50 = (bf16[48,12]{0,1:T(8,128)(2,1)S(1)}, bf16[48,12]{0,1:T(8,128)(2,1)}, u32[]{:S(2)}) copy-start(bf16[48,12]{0,1:T(8,128)(2,1)} %param.24) | copy-start | bytes 3460
  7.2 31.9 %copy-start.31 = (bf16[48,256]{1,0:T(8,128)(2,1)S(1)}, bf16[48,256]{1,0:T(8,128)(2,1)}, u32[]{:S(2)}) copy-start(bf16[48,256]{1,0:T(8,128)(2,1)} %param.23) | copy-start | bytes 73732
  7.2 50.6 %copy-start.55 = (f32[12]{0:T(128)S(1)}, f32[12]{0:T(128)}, u32[]{:S(2)}) copy-start(f32[12]{0:T(128)} %param.29) | copy-start | bytes 148
  7.3 50.6 %all-gather.7.cloned.1.call-start = ((), (), s32[]{:S(2)}) async-start(), calls=%async_computation.6 | async-start | bytes 2359296 | tf_op jit(solution)/shard_map/all_gather | solution.py:124
  12.1 74.6 %all-gather.9.cloned.1.call-start = ((), (), s32[]{:S(2)}) async-start(), calls=%async_computation.7 | async-start | bytes 2506752 | tf_op jit(solution)/shard_map/all_gather | solution.py:126
  12.9 228.0 %all-gather.13.cloned.1.call-start = ((), (), s32[]{:S(2)}) async-start(), calls=%async_computation.14 | async-start | bytes 2359296 | tf_op jit(solution)/shard_map/all_gather | solution.py:158
  13.6 50.2 %copy-start.54 = (f32[256]{0:T(256)S(1)}, f32[256]{0:T(256)}, u32[]{:S(2)}) copy-start(f32[256]{0:T(256)} %param.28) | copy-start | bytes 3076
  13.6 227.3 %all-gather.11.cloned.1.call-start = ((), (), s32[]{:S(2)}) async-start(), calls=%async_computation.8 | async-start | bytes 1253376 | tf_op jit(solution)/shard_map/all_gather | solution.py:129
  14.2 476.2 %reduce-scatter.13.cloned.1.call-start = ((), (), s32[]{:S(2)}) async-start(), calls=%async_computation.11 | async-start | bytes 786432 | tf_op jit(solution)/shard_map/reduce_scatter | solution.py:179
  14.9 45.6 %copy-start.52 = (f32[12]{0:T(128)}, f32[12]{0:T(128)S(1)}, u32[]{:S(2)}) copy-start(f32[12]{0:T(128)S(1)} %exponential_negate_fusion) | copy-start | bytes 148
  14.9 50.5 %copy-start.40 = (f32[1,256]{1,0:T(1,128)}, f32[1,256]{1,0:T(1,128)S(1)}, u32[]{:S(2)}) copy-start(f32[1,256]{1,0:T(1,128)S(1)} %get-tuple-element.642) | copy-start | bytes 3076
  15.0 50.5 %copy-start.42 = (f32[1,256]{1,0:T(1,128)}, f32[1,256]{1,0:T(1,128)S(1)}, u32[]{:S(2)}) copy-start(f32[1,256]{1,0:T(1,128)S(1)} %get-tuple-element.643) | copy-start | bytes 3076
  15.0 50.5 %copy-start.44 = (f32[1,256]{1,0:T(1,128)}, f32[1,256]{1,0:T(1,128)S(1)}, u32[]{:S(2)}) copy-start(f32[1,256]{1,0:T(1,128)S(1)} %get-tuple-element.644) | copy-start | bytes 3076
  15.0 50.5 %copy-start.46 = (f32[1,256]{1,0:T(1,128)}, f32[1,256]{1,0:T(1,128)S(1)}, u32[]{:S(2)}) copy-start(f32[1,256]{1,0:T(1,128)S(1)} %get-tuple-element.645) | copy-start | bytes 3076
  39.1 26.3 %copy-start.26 = (bf16[768,12]{0,1:T(8,128)(2,1)}, bf16[768,12]{0,1:T(8,128)(2,1)S(1)}, u32[]{:S(2)}) copy-start(bf16[768,12]{0,1:T(8,128)(2,1)S(1)} %reshape.424) | copy-start | bytes 55300
  70.5 19.8 %copy-start.7 = (bf16[1024,768]{1,0:T(8,128)(2,1)S(1)}, bf16[1024,768]{1,0:T(8,128)(2,1)}, u32[]{:S(2)}) copy-start(bf16[1024,768]{1,0:T(8,128)(2,1)} %all-gather.7.cloned.1.call-done) | copy-start | bytes 4718596
  230.8 10.1 %copy-start.49 = (f32[768]{0:T(1024)S(1)}, f32[768]{0:T(1024)}, u32[]{:S(2)}) copy-start(f32[768]{0:T(1024)} %param.32) | copy-start | bytes 9220
  240.9 238.3 %copy-start.36 = (f32[1024]{0:T(1024)}, f32[1024]{0:T(1024)S(1)}, u32[]{:S(2)}) copy-start(f32[1024]{0:T(1024)S(1)} %get-tuple-element.641) | copy-start | bytes 12292
  440.6 74.2 %reduce-scatter.19.cloned.1.call-start = ((), (), s32[]{:S(2)}) async-start(), calls=%async_computation.15 | async-start | bytes 208896
  445.3 8.1 %copy-start.53 = (f32[12]{0:T(128)S(1)}, f32[12]{0:T(128)}, u32[]{:S(2)}) copy-start(f32[12]{0:T(128)} %copy-done.52) | copy-start | bytes 148
  445.3 8.8 %copy-start.8 = (bf16[1024,768]{1,0:T(8,128)(2,1)S(1)}, bf16[1024,768]{1,0:T(8,128)(2,1)}, u32[]{:S(2)}) copy-start(bf16[1024,768]{1,0:T(8,128)(2,1)} %all-gather.7.cloned.1.call-done) | copy-start | bytes 4718596
  445.3 10.0 %copy-start.30 = (f32[768]{0:T(1024)S(1)}, f32[768]{0:T(1024)}, u32[]{:S(2)}) copy-start(f32[768]{0:T(1024)} %get-tuple-element.542) | copy-start | bytes 9220
  462.0 154.9 %all-reduce.27.cloned.1.call-start = ((), (), s32[]{:S(2)}) async-start(), calls=%async_computation.16 | async-start | bytes 4718592
  479.2 199.2 %reduce-scatter.17.cloned.1.call-start = ((), (), s32[]{:S(2)}) async-start(), calls=%async_computation.13 | async-start | bytes 1253376 | tf_op jit(solution)/shard_map/reduce_scatter | solution.py:200
  483.3 223.1 %reduce-scatter.11.cloned.1.call-start = ((), (), s32[]{:S(2)}) async-start(), calls=%async_computation.10 | async-start | bytes 2359296 | tf_op jit(solution)/shard_map/reduce_scatter | solution.py:176
  490.4 280.5 %reduce-scatter.15.cloned.1.call-start = ((), (), s32[]{:S(2)}) async-start(), calls=%async_computation.12 | async-start | bytes 417792 | tf_op jit(solution)/shard_map/reduce_scatter | solution.py:197
  492.8 8.2 %copy-start.38 = (f32[768]{0:T(1024)S(1)}, f32[768]{0:T(1024)}, u32[]{:S(2)}) copy-start(f32[768]{0:T(1024)} %get-tuple-element.531) | copy-start | bytes 9220
  492.9 213.5 %copy-start.22 = (bf16[768,256]{1,0:T(8,128)(2,1)S(1)}, bf16[768,256]{1,0:T(8,128)(2,1)}, u32[]{:S(2)}) copy-start(bf16[768,256]{1,0:T(8,128)(2,1)} %copy-done.21) | copy-start | bytes 1179652
  492.9 213.5 %copy-start.33 = (f32[512]{0:T(512)S(1)}, f32[512]{0:T(512)}, u32[]{:S(2)}) copy-start(f32[512]{0:T(512)} %copy-done.32) | copy-start | bytes 6148
  492.9 300.2 %reduce-scatter.9.cloned.1.call-start = ((), (), s32[]{:S(2)}) async-start(), calls=%async_computation.9 | async-start | bytes 2359296 | tf_op jit(solution)/shard_map/reduce_scatter | solution.py:151
  496.9 296.2 %copy-start.13 = (bf16[1,512,768]{2,1,0:T(8,128)(2,1)S(1)}, bf16[1,512,768]{2,1,0:T(8,128)(2,1)}, u32[]{:S(2)}) copy-start(bf16[1,512,768]{2,1,0:T(8,128)(2,1)} %param.19) | copy-start | bytes 2359300
  496.9 296.2 %copy-start.15 = (bf16[1,512,768]{2,1,0:T(8,128)(2,1)S(1)}, bf16[1,512,768]{2,1,0:T(8,128)(2,1)}, u32[]{:S(2)}) copy-start(bf16[1,512,768]{2,1,0:T(8,128)(2,1)} %param.20) | copy-start | bytes 2359300
  (37 other events, 147.9 us)
Sparse Core Ops, SparseCore 0:
  12.2 29.8 all-gather.6
  44.5 42.2 all-gather.8
  88.3 25.9 all-gather.12
  116.5 38.3 all-gather.10
  440.7 13.3 reduce-scatter.12
  462.1 52.6 reduce-scatter.18
  518.8 98.0 all-reduce.26
  620.9 57.3 reduce-scatter.16
  681.2 25.0 reduce-scatter.10
  709.7 55.5 reduce-scatter.14
  767.6 25.4 reduce-scatter.8
where the time goes:
time: 811 us; the launch traced here: 803 us
  local copies, waits for them, and re-layouts  244 us (30%)
  waiting for transfers between devices  226 us (28%)
  blocking collectives  122 us (15%)
  matrix products  106 us (13%)
  other arithmetic  87.3 us (11%)
  between operations  15.4 us (2%)
    dynamic_update_slice x24, local copies, waits for them, and re-layouts, scan_heads(): lax.scan(jax.checkpoint(scan_block), start_state, blocks)  150 us
    unnamed x13, waiting for transfers between devices  113 us
    psum x1, blocking collectives, on_device(): lax.psum((grad_conv_inner, grad_bias_inner, grad_step_bias, grad_log_deca...  61.8 us
    reduce_scatter x1, waiting for transfers between devices, on_device(): lax.psum_scatter(grad_out.astype(jnp.bfloat16), 'dp', scatter_dimension=1...  59.7 us
    dot_general x12, matrix products, scan_block(): intra_out = jnp.einsum('hij,jhp->ihp', weights, scaled_in, precision=NEARLY)  31.1 us
    dot_general x8, matrix products, contract(): lax.dot_general(left, right, (((left_dim,), (right_dim,)), ((), ())), pre...  27.1 us
    reduce_scatter x1, waiting for transfers between devices, on_device(): lax.psum_scatter(d_partial.astype(jnp.bfloat16), 'tensor', scatter_dimens...  26.5 us
    all_gather x1, blocking collectives, on_device(): lax.all_gather(proj_dt, 'dp', axis=0, tiled=True)  23.2 us
  transfers between devices with their start and end apart: 11, of which 6 were waited for; matrix products, arithmetic and copies ran while one was open for 29% of the time, Pallas kernels for 0%

commit v1 on v0

v1 whole, which is shorter than its diff:
```python
import functools

import jax
import jax.numpy as jnp
from jax import lax
from jax.experimental import pallas as pl
from jax.experimental.pallas import tpu as pltpu
from jax.sharding import PartitionSpec as P

NSTATE = 128
SPAN = 256
INNER = 1536
PAD = 128
EPSILON = 1e-05
F32 = jnp.float32
BF16 = jnp.bfloat16
VMEM_LIMIT = 60 * 1024 * 1024


def mm(left, right, left_dim=1, right_dim=0):
    return lax.dot_general(
        left, right, (((left_dim,), (right_dim,)), ((), ())), preferred_element_type=F32
    )


def exact_mm(left, right):
    return lax.dot_general(
        left, right, (((1,), (0,)), ((), ())), preferred_element_type=F32,
        precision=lax.Precision.HIGHEST,
    )


def sigmoid(v):
    return 1.0 / (1.0 + jnp.exp(-v))


def iotas(size):
    return (
        lax.broadcasted_iota(jnp.int32, (size, size), 0),
        lax.broadcasted_iota(jnp.int32, (size, size), 1),
    )


def by_pair(values, pair, first_lanes):
    left = values[:, 2 * pair : 2 * pair + 1]
    right = values[:, 2 * pair + 1 : 2 * pair + 2]
    return jnp.where(first_lanes, left, right)


def steps_of(step_raw, hp):
    shifted = step_raw + hp[0:1, :]
    step = jnp.maximum(shifted, 0.0) + jnp.log1p(jnp.exp(-jnp.abs(shifted)))
    return shifted, step, -jnp.exp(hp[1:2, :]) * step


def forward_kernel(
    normed_ref, cot_ref, wcat_ref, out_ref, cw_ref, hp_ref, ch_ref,
    raw_ref, conv_ref, scanned_ref, gated_ref, state_out_ref, dng_ref, stats_ref,
    buf, state, fresh_in,
):
    at = pl.program_id(0)
    span = normed_ref.shape[0]
    width = scanned_ref.shape[1]
    both = width + 2 * NSTATE

    @pl.when(at == 0)
    def _():
        buf[0:8, :] = jnp.zeros((8, both), F32)
        state[...] = jnp.zeros_like(state)

    @pl.when(at > 0)
    def _():
        buf[0:8, :] = buf[span : span + 8, :]

    raw_ref[...] = mm(normed_ref[...], wcat_ref[...])
    buf[8 : 8 + span, :] = raw_ref[:, width : width + both]
    conv = cw_ref[4:5, :] + cw_ref[0:1, :] * buf[5 : 5 + span, :]
    for tap in range(1, 4):
        conv = conv + cw_ref[tap : tap + 1, :] * buf[5 + tap : 5 + tap + span, :]
    conv_ref[...] = conv
    act = (conv * sigmoid(conv)).astype(BF16)
    km = act[:, width : width + NSTATE]
    qm = act[:, width + NSTATE :]
    shifted, step, rate = steps_of(raw_ref[:, width + both :], hp_ref[...])
    rows, cols = iotas(span)
    causal = cols <= rows
    cum = exact_mm(jnp.where(causal, 1.0, 0.0), rate)
    cum_t = cum.T
    grow = jnp.exp(cum)
    last = cum[span - 1 : span, :]
    tail = jnp.exp(last - cum)
    total = jnp.exp(last)
    scores = jnp.where(causal, mm(qm, km, 1, 1), 0.0)
    state_now = state[...]
    state_out_ref[...] = state_now
    inter = mm(qm, state_now.astype(BF16))
    first = lax.broadcasted_iota(jnp.int32, (span, 128), 1) < 64
    for pair in range(width // 128):
        lanes = slice(pair * 128, pair * 128 + 128)
        x = act[:, lanes].astype(F32)
        u = x * by_pair(step, pair, first)
        fresh_in[:, lanes] = (u * by_pair(tail, pair, first)).astype(BF16)
        low_u = u.astype(BF16)
        ys = []
        for head in (2 * pair, 2 * pair + 1):
            gap = jnp.minimum(cum[:, head : head + 1] - cum_t[head : head + 1, :], 0.0)
            ys.append(mm((jnp.exp(gap) * scores).astype(BF16), low_u))
        y = jnp.where(first, ys[0], ys[1]) + inter[:, lanes] * by_pair(grow, pair, first)
        scanned_ref[:, lanes] = y + ch_ref[0:1, lanes] * x
    fresh = mm(km, fresh_in[...], 0, 0)
    for pair in range(width // 128):
        lanes = slice(pair * 128, pair * 128 + 128)
        state[:, lanes] = (
            by_pair(total, pair, first[0:1]) * state_now[:, lanes] + fresh[:, lanes]
        )
    gate_z = raw_ref[:, 0:width]
    gated = scanned_ref[...] * (gate_z * sigmoid(gate_z))
    gated_ref[...] = gated
    dng = mm(cot_ref[...], out_ref[...])
    dng_ref[...] = dng
    squares = jnp.sum(gated * gated, axis=1, keepdims=True)
    cross = jnp.sum(dng * ch_ref[1:2, :] * gated, axis=1, keepdims=True)
    lane = lax.broadcasted_iota(jnp.int32, (span, PAD), 1)
    stats_ref[...] = jnp.where(lane == 0, squares, jnp.where(lane == 1, cross, 0.0))


def backward_kernel(
    normed_ref, raw_ref, conv_ref, scanned_ref, state_ref, dng_ref, stats_ref,
    wcat_ref, cw_ref, hp_ref, ch_ref, sum_ref,
    partial_ref, grads_ref, gcw_ref, ghp_ref, gch_ref,
    adjoint, buf, acc, dye, ut, dz, prod, score_sum,
):
    at = pl.program_id(0)
    span = normed_ref.shape[0]
    width = scanned_ref.shape[1]
    both = width + 2 * NSTATE

    @pl.when(at == 0)
    def _():
        buf[span : span + 8, :] = jnp.zeros((8, both), F32)
        adjoint[...] = jnp.zeros_like(adjoint)
        acc[...] = jnp.zeros_like(acc)
        gcw_ref[...] = jnp.zeros_like(gcw_ref)
        ghp_ref[...] = jnp.zeros_like(ghp_ref)
        gch_ref[...] = jnp.zeros_like(gch_ref)

    @pl.when(at > 0)
    def _():
        buf[span : span + 8, :] = buf[0:8, :]

    stats = stats_ref[...]
    scale = lax.rsqrt(stats[:, 0:1] / INNER + EPSILON)
    pull = scale * scale * scale * stats[:, 1:2] / INNER
    gate_z = raw_ref[:, 0:width]
    sig = sigmoid(gate_z)
    silu = gate_z * sig
    scanned = scanned_ref[...]
    gated = scanned * silu
    dng = dng_ref[...]
    d_gated = scale * (dng * ch_ref[1:2, :]) - gated * pull
    gch_ref[1:2, :] += jnp.sum(dng * gated * scale, axis=0, keepdims=True)
    dy = d_gated * silu
    dz[:, 0:width] = (d_gated * scanned * (sig * (1.0 + gate_z * (1.0 - sig)))).astype(BF16)

    conv = conv_ref[...]
    sig_conv = sigmoid(conv)
    act = (conv * sig_conv).astype(BF16)
    slope = sig_conv * (1.0 + conv * (1.0 - sig_conv))
    km = act[:, width : width + NSTATE]
    qm = act[:, width + NSTATE :]
    hp = hp_ref[...]
    shifted, step, rate = steps_of(raw_ref[:, width + both :], hp)
    rows, cols = iotas(span)
    causal = cols <= rows
    cum = exact_mm(jnp.where(causal, 1.0, 0.0), rate)
    cum_t = cum.T
    grow = jnp.exp(cum)
    last = cum[span - 1 : span, :]
    tail = jnp.exp(last - cum)
    total = jnp.exp(last)
    scores = mm(qm, km, 1, 1)
    state = state_ref[...]
    low_state = state.astype(BF16)
    adj = adjoint[...]
    low_adj = adj.astype(BF16)
    inter = mm(qm, low_state)
    du_state = mm(km, low_adj)
    first = lax.broadcasted_iota(jnp.int32, (span, 128), 1) < 64
    lane = lax.broadcasted_iota(jnp.int32, (span, PAD), 1)
    row_sums = jnp.zeros((span, PAD), F32)
    col_sums = []
    for pair in range(width // 128):
        lanes = slice(pair * 128, pair * 128 + 128)
        x = act[:, lanes].astype(F32)
        step_pair = by_pair(step, pair, first)
        tail_pair = by_pair(tail, pair, first)
        u = x * step_pair
        low_u = u.astype(BF16)
        u_tail = u * tail_pair
        ut[:, lanes] = u_tail.astype(BF16)
        dy_pair = dy[:, lanes]
        low_dy = dy_pair.astype(BF16)
        dy_grow = dy_pair * by_pair(grow, pair, first)
        dye[:, lanes] = dy_grow.astype(BF16)
        prod[0:span, lanes] = dy_grow * inter[:, lanes]
        prod[span : 2 * span, lanes] = u_tail * du_state[:, lanes]
        dus = []
        for head in (2 * pair, 2 * pair + 1):
            mine = first if head % 2 == 0 else jnp.logical_not(first)
            d_weights = mm(jnp.where(mine, low_dy, jnp.zeros_like(low_dy)), low_u, 1, 1)
            gap = cum[:, head : head + 1] - cum_t[head : head + 1, :]
            table = jnp.exp(jnp.where(causal, gap, -1e30))
            weights = table * scores
            d_scores = table * d_weights
            if head == 0:
                score_sum[...] = d_scores
            else:
                score_sum[...] += d_scores
            moved = weights * d_weights
            row_sums = jnp.where(
                lane == head, jnp.sum(moved, axis=1, keepdims=True), row_sums
            )
            col_sums.append(jnp.sum(moved, axis=0, keepdims=True))
            dus.append(mm(weights.astype(BF16), low_dy, 0, 0))
        du = jnp.where(first, dus[0], dus[1]) + du_state[:, lanes] * tail_pair
        prod[2 * span : 3 * span, lanes] = x * du
        gch_ref[0:1, lanes] += jnp.sum(dy_pair * x, axis=0, keepdims=True)
        dx = step_pair * du + ch_ref[0:1, lanes] * dy_pair
        buf[0:span, lanes] = dx * slope[:, lanes]
    col_sums.append(jnp.zeros((PAD - len(col_sums), span), F32))
    col_sums = jnp.concatenate(col_sums, axis=0).T
    prods = prod[...]
    high = prods.astype(BF16)
    low = (prods - high.astype(F32)).astype(BF16)
    summer = sum_ref[...]
    heads = mm(high, summer) + mm(low, summer)
    met = jnp.sum(adj * state, axis=0, keepdims=True)
    met = jnp.broadcast_to(met, (8, width))
    met_high = met.astype(BF16)
    met_low = (met - met_high.astype(F32)).astype(BF16)
    met = (mm(met_high, summer) + mm(met_low, summer))[0:1, :]
    d_rate = (
        exact_mm(jnp.where(cols >= rows, 1.0, 0.0), row_sums - col_sums + heads[0:span])
        + exact_mm(jnp.where(cols < rows, 1.0, 0.0), heads[span : 2 * span])
        + total * met
    )
    d_step = heads[2 * span :] - jnp.exp(hp[1:2, :]) * d_rate
    d_step_raw = d_step * sigmoid(shifted)
    ghp_ref[0:1, :] += jnp.sum(d_step_raw, axis=0, keepdims=True)
    ghp_ref[1:2, :] += jnp.sum(d_rate * rate, axis=0, keepdims=True)
    dz[:, width + both :] = d_step_raw.astype(BF16)

    low_sum = score_sum[...].astype(BF16)
    dk = mm(low_sum, qm, 0, 0) + mm(ut[...], low_adj, 1, 1)
    dq = mm(low_sum, km) + mm(dye[...], low_state, 1, 1)
    buf[0:span, width : width + NSTATE] = dk * slope[:, width : width + NSTATE]
    buf[0:span, width + NSTATE : both] = dq * slope[:, width + NSTATE :]
    raw = raw_ref[:, width : width + both]
    gcw_ref[4:5, :] += jnp.sum(buf[0:span, :], axis=0, keepdims=True)
    d_raw = jnp.zeros((span, both), F32)
    for tap in range(4):
        moved = buf[3 - tap : 3 - tap + span, :]
        d_raw = d_raw + cw_ref[tap : tap + 1, :] * moved
        gcw_ref[tap : tap + 1, :] += jnp.sum(raw * moved, axis=0, keepdims=True)
    dz[:, width : width + both] = d_raw.astype(BF16)

    low_dz = dz[...]
    partial_ref[...] = mm(low_dz, wcat_ref[...], 1, 1).astype(BF16)
    acc[...] += mm(normed_ref[...], low_dz, 0, 0)
    fresh = mm(qm, dye[...], 0, 0)
    for pair in range(width // 128):
        lanes = slice(pair * 128, pair * 128 + 128)
        adjoint[:, lanes] = by_pair(total, pair, first[0:1]) * adj[:, lanes] + fresh[:, lanes]

    @pl.when(at == pl.num_programs(0) - 1)
    def _():
        grads_ref[...] = acc[...].astype(BF16)


def forward_part(normed, cot, wcat, out_t, cw, hp, ch):
    length, model = normed.shape
    width = ch.shape[1]
    both = width + 2 * NSTATE
    cat = wcat.shape[1]
    blocks = length // SPAN
    row = lambda cols: pl.BlockSpec((SPAN, cols), lambda i: (i, 0))
    whole = lambda arr: pl.BlockSpec(arr.shape, lambda i: (0, 0))
    shape = lambda r, c: jax.ShapeDtypeStruct((r, c), F32)
    return pl.pallas_call(
        forward_kernel,
        grid=(blocks,),
        in_specs=[row(model), row(model), whole(wcat), whole(out_t), whole(cw), whole(hp), whole(ch)],
        out_specs=[
            row(cat), row(both), row(width), row(width),
            pl.BlockSpec((NSTATE, width), lambda i: (i, 0)), row(width), row(PAD),
        ],
        out_shape=[
            shape(length, cat), shape(length, both), shape(length, width), shape(length, width),
            shape(blocks * NSTATE, width), shape(length, width), shape(length, PAD),
        ],
        scratch_shapes=[
            pltpu.VMEM((SPAN + 8, both), F32),
            pltpu.VMEM((NSTATE, width), F32),
            pltpu.VMEM((SPAN, width), BF16),
        ],
        compiler_params=pltpu.CompilerParams(vmem_limit_bytes=VMEM_LIMIT),
        cost_estimate=pl.CostEstimate(
            flops=2 * length * (model * (cat + width) + 4 * SPAN * width),
            bytes_accessed=25 * 2**20, transcendentals=length * width * 6,
        ),
        name="mixer_forward",
    )(normed, cot, wcat, out_t, cw, hp, ch)


def backward_part(normed, raw, conv, scanned, states, dng, stats, wcat, cw, hp, ch):
    length, model = normed.shape
    width = ch.shape[1]
    both = width + 2 * NSTATE
    cat = wcat.shape[1]
    blocks = length // SPAN
    summer = (
        lax.broadcasted_iota(jnp.int32, (width, PAD), 0) // 64
        == lax.broadcasted_iota(jnp.int32, (width, PAD), 1)
    ).astype(BF16)
    row = lambda cols: pl.BlockSpec((SPAN, cols), lambda i: (blocks - 1 - i, 0))
    whole = lambda arr: pl.BlockSpec(arr.shape, lambda i: (0, 0))
    return pl.pallas_call(
        backward_kernel,
        grid=(blocks,),
        in_specs=[
            row(model), row(cat), row(both), row(width),
            pl.BlockSpec((NSTATE, width), lambda i: (blocks - 1 - i, 0)), row(width), row(PAD),
            whole(wcat), whole(cw), whole(hp), whole(ch), whole(summer),
        ],
        out_specs=[row(model), whole(wcat), whole(cw), whole(hp), whole(ch)],
        out_shape=[
            jax.ShapeDtypeStruct((length, model), BF16),
            jax.ShapeDtypeStruct((model, cat), BF16),
            jax.ShapeDtypeStruct(cw.shape, F32),
            jax.ShapeDtypeStruct(hp.shape, F32),
            jax.ShapeDtypeStruct(ch.shape, F32),
        ],
        scratch_shapes=[
            pltpu.VMEM((NSTATE, width), F32),
            pltpu.VMEM((SPAN + 8, both), F32),
            pltpu.VMEM((model, cat), F32),
            pltpu.VMEM((SPAN, width), BF16),
            pltpu.VMEM((SPAN, width), BF16),
            pltpu.VMEM((SPAN, cat), BF16),
            pltpu.VMEM((3 * SPAN, width), F32),
            pltpu.VMEM((SPAN, SPAN), F32),
        ],
        compiler_params=pltpu.CompilerParams(vmem_limit_bytes=VMEM_LIMIT),
        cost_estimate=pl.CostEstimate(
            flops=2 * length * (2 * model * cat + 10 * SPAN * width),
            bytes_accessed=25 * 2**20, transcendentals=length * width * 8,
        ),
        name="mixer_adjoint",
    )(normed, raw, conv, scanned, states, dng, stats, wcat, cw, hp, ch, summer)


def swap(values, bit, axis, size):
    return lax.ppermute(values, axis, [(i, i ^ bit) for i in range(size)])


def scatter_sum(values, size, order):
    me = lax.axis_index("dp")
    bits = size.bit_length() - 1
    rows = values.shape[0] // size
    held = values.reshape((2,) * bits + (rows, values.shape[1]))
    left = list(range(bits - 1, -1, -1))
    for bit in order:
        axis = left.index(bit)
        mine = (me >> bit) & 1
        keep = lax.dynamic_index_in_dim(held, mine, axis, keepdims=False)
        send = lax.dynamic_index_in_dim(held, 1 - mine, axis, keepdims=False)
        got = swap(send, 1 << bit, "dp", size)
        held = (keep.astype(F32) + got.astype(F32)).astype(BF16)
        left.pop(axis)
    return held


def whole_sum(values, axis, size):
    bit = 1
    while bit < size:
        values = values + swap(values, bit, axis, size)
        bit *= 2
    return values


def token_scatter(values, size):
    if size != 2:
        return lax.psum_scatter(values, "tensor", scatter_dimension=0, tiled=True).astype(F32)
    me = lax.axis_index("tensor")
    half = values.shape[0] // 2
    keep = lax.dynamic_slice_in_dim(values, me * half, half, 0)
    send = lax.dynamic_slice_in_dim(values, (1 - me) * half, half, 0)
    return keep.astype(F32) + swap(send, 1, "tensor", 2).astype(F32)


def on_device(
    dp, tp,
    tokens, cotangent, norm_in, gate_inner_projection, proj_bc, proj_dt, conv_inner,
    bias_inner, conv_bc, bias_bc, step_bias, log_decay, skip_gain, norm_gate, proj_out,
):
    width = gate_inner_projection.shape[2]
    heads = step_bias.shape[0]
    model = tokens.shape[2]
    share = model // dp
    cat = 2 * width + 2 * NSTATE + PAD
    packed = jnp.concatenate(
        [
            gate_inner_projection.reshape(share, 2 * width),
            proj_bc,
            jnp.pad(proj_dt, ((0, 0), (0, PAD - heads))),
            proj_out.T,
        ],
        axis=1,
    )
    weights = lax.all_gather(packed, "dp", axis=0, tiled=True)
    wcat, out_t = weights[:, :cat], weights[:, cat:]
    token_rows = tokens[0].astype(F32)
    inv_rms = lax.rsqrt(jnp.mean(token_rows * token_rows, axis=-1, keepdims=True) + EPSILON)
    local_normed = (token_rows * inv_rms * norm_in).astype(BF16)
    normed = lax.all_gather(local_normed, "tensor", axis=0, tiled=True)
    cot = lax.all_gather(cotangent[0], "tensor", axis=0, tiled=True)
    cw = jnp.pad(
        jnp.concatenate(
            [
                jnp.concatenate([conv_inner, conv_bc], axis=1),
                jnp.concatenate([bias_inner, bias_bc])[None],
            ],
            axis=0,
        ),
        ((0, 3), (0, 0)),
    )
    hp = jnp.pad(jnp.stack([step_bias, log_decay]), ((0, 6), (0, PAD - heads)))
    ch = jnp.pad(jnp.stack([jnp.repeat(skip_gain, width // heads), norm_gate]), ((0, 6), (0, 0)))
    raw, conv, scanned, gated, states, dng, stats = forward_part(
        normed, cot, wcat, out_t, cw, hp, ch
    )
    stats = jnp.pad(
        whole_sum(stats[:, :2].T, "tensor", tp).T, ((0, 0), (0, PAD - 2))
    )
    scale = lax.rsqrt(stats[:, 0:1] / INNER + EPSILON)
    gate_normed = (gated * scale * norm_gate).astype(BF16)
    branch = token_scatter(mm(gate_normed, out_t, 1, 1).astype(BF16), tp)
    block_out = (token_rows + branch).astype(BF16)[None]
    bits = dp.bit_length() - 1
    order = tuple(range(bits))
    other = (0,) + tuple(range(2, bits)) + (1,)
    grad_out = scatter_sum(mm(cot, gate_normed, 0, 0).astype(BF16), dp, other)
    partial, grads, gcw, ghp, gch = backward_part(
        normed, raw, conv, scanned, states, dng, stats, wcat, cw, hp, ch
    )
    cut = cat // 256 * 128
    grads = jnp.concatenate(
        [scatter_sum(grads[:, :cut], dp, order), scatter_sum(grads[:, cut:], dp, other)], axis=1
    )
    d_rows = token_scatter(partial, tp)
    gained = norm_in * d_rows
    dotted = jnp.sum(token_rows * gained, axis=-1, keepdims=True)
    input_grad = (
        cotangent[0].astype(F32)
        + inv_rms * gained
        - token_rows * (inv_rms * inv_rms * inv_rms * dotted / model)
    )[None]
    grad_norm_in = jnp.sum(d_rows * token_rows * inv_rms, axis=0)
    grad_skip = jnp.sum(gch[0].reshape(heads, -1), axis=1)
    mine = [gcw[:5, :width].reshape(-1), ghp[0, :heads], ghp[1, :heads], grad_skip, gch[1]]
    common = [gcw[:5, width:].reshape(-1), grad_norm_in]
    sizes = [v.shape[0] for v in mine + common]
    flat = jnp.concatenate(mine + common)
    count = flat.shape[0]
    flat = jnp.pad(flat, (0, -count % 1024)).reshape(-1, 128)
    flat = whole_sum(flat, "dp", dp).reshape(-1)[:count]
    own = sum(sizes[: len(mine)])
    grad_bc = grads[:, 2 * width : 2 * width + 2 * NSTATE].astype(F32)
    shared = jnp.concatenate([grad_bc.reshape(-1), flat[own:]])
    shared = whole_sum(shared.reshape(-1, 128), "tensor", tp).reshape(-1)
    grad_bc = shared[: grad_bc.size].reshape(grad_bc.shape)
    shared = shared[grad_bc.size :]
    parts = jnp.split(flat[:own], [sum(sizes[:i]) for i in range(1, len(mine))])
    gconv = parts[0].reshape(5, width)
    gbc = shared[: sizes[len(mine)]].reshape(5, 2 * NSTATE)
    return (
        block_out,
        input_grad,
        shared[sizes[len(mine)] :],
        grads[:, : 2 * width].astype(F32).reshape(share, 2, width),
        grad_bc,
        grads[:, 2 * width + 2 * NSTATE :][:, :heads].astype(F32),
        gconv[:4],
        gconv[4],
        gbc[:4],
        gbc[4],
        parts[1],
        parts[2],
        parts[3],
        parts[4],
        grad_out.T.astype(F32),
    )


def solution(mesh):
    placed = (
        P("dp", "tensor", None),
        P("dp", "tensor", None),
        P(),
        P("dp", None, "tensor"),
        P("dp", None),
        P("dp", "tensor"),
        P(None, "tensor"),
        P("tensor"),
        P(),
        P(),
        P("tensor"),
        P("tensor"),
        P("tensor"),
        P("tensor"),
        P("tensor", "dp"),
    )
    return jax.shard_map(
        functools.partial(on_device, mesh.shape["dp"], mesh.shape["tensor"]),
        mesh=mesh,
        in_specs=placed,
        out_specs=(
            P("dp", "tensor", None),
            P("dp", "tensor", None),
            P(),
            P("dp", None, "tensor"),
            P("dp", None),
            P("dp", "tensor"),
            P(None, "tensor"),
            P("tensor"),
            P(),
            P(),
            P("tensor"),
            P("tensor"),
            P("tensor"),
            P("tensor"),
            P("tensor", "dp"),
        ),
        check_vma=False,
    )
```

time: 811 us -> 322 us (0.40)
  local copies, waits for them, and re-layouts: 244 us -> 30.3 us
  blocking collectives: 122 us -> 0 us
  matrix products: 106 us -> 6.76 us
  other arithmetic: 87.3 us -> 16 us
  Pallas kernels: 0 us -> 67.5 us
  waiting for transfers between devices: 226 us -> 168 us
  starting transfers between devices: 0.45 us -> 18.7 us
    dynamic_update_slice x24 -> x0, local copies, waits for them, and re-layouts: 150 us -> none  [scan_heads(): lax.scan(jax.checkpoint(scan_block), start_state, blocks)]
    unnamed x13 -> x3, waiting for transfers between devices: 113 us -> 0.73 us
    dot_general x68 -> x2, matrix products: 106 us -> 6.76 us  [mm(): lax.dot_general(left, right, (((left_dim,), (right_dim,)), ((), ())), pre...]
    reduce_scatter x5 -> x0, waiting for transfers between devices: 96.5 us -> none  [the longest x1 59.7 us: on_device(): lax.psum_scatter(grad_out.astype(jnp.bfloat16), 'dp', scatter_dimension=1...]
    all_gather x4 -> x3, waiting for transfers between devices: 16.3 us -> 99.5 us  [the longest x1 48.8 us: on_device(): weights = lax.all_gather(packed, 'dp', axis=0, tiled=True)]
    psum x4 -> x0, blocking collectives: 80.3 us -> none  [the longest x1 61.8 us: on_device(): lax.psum((grad_conv_inner, grad_bias_inner, grad_step_bias, grad_log_deca...]
    ppermute x0 -> x20, waiting for transfers between devices: none -> 67.8 us  [swap(): return lax.ppermute(values, axis, [(i, i ^ bit) for i in range(size)])]
    pallas_call x0 -> x2, Pallas kernels: none -> 67.5 us  [the longest x1 44 us: backward_part(): pl.pallas_call(backward_kernel, grid=(blocks,), in_specs=[row(model), row...]
  transfers between devices with their start and end apart: 11 -> 23, of which waited for: 6 -> 15; matrix products, arithmetic and copies ran while one was open for 29% -> 10% of each run, Pallas kernels for 0% -> 0%
where the time goes in v1:
time: 322 us
  waiting for transfers between devices  168 us (52%)
  Pallas kernels  67.5 us (21%)
  local copies, waits for them, and re-layouts  30.3 us (9%)
  starting transfers between devices  18.7 us (6%)
  other arithmetic  16 us (5%)
  between operations  14.4 us (4%)
  matrix products  6.76 us (2%)
    ppermute x20, waiting for transfers between devices, swap(): return lax.ppermute(values, axis, [(i, i ^ bit) for i in range(size)])  67.8 us
    all_gather x1, waiting for transfers between devices, on_device(): weights = lax.all_gather(packed, 'dp', axis=0, tiled=True)  48.8 us
    pallas_call x1, Pallas kernels, backward_part(): pl.pallas_call(backward_kernel, grid=(blocks,), in_specs=[row(model), row...  44 us
    all_gather x1, waiting for transfers between devices, on_device(): normed = lax.all_gather(local_normed, 'tensor', axis=0, tiled=True)  29.4 us
    pallas_call x1, Pallas kernels, forward_part(): pl.pallas_call(forward_kernel, grid=(blocks,), in_specs=[row(model), row(...  23.4 us
    all_gather x1, waiting for transfers between devices, on_device(): cot = lax.all_gather(cotangent[0], 'tensor', axis=0, tiled=True)  21.3 us
    ppermute x20, starting transfers between devices, swap(): return lax.ppermute(values, axis, [(i, i ^ bit) for i in range(size)])  18.6 us
    dot_general x2, matrix products, mm(): lax.dot_general(left, right, (((left_dim,), (right_dim,)), ((), ())), pre...  6.76 us
  transfers between devices with their start and end apart: 23, of which 15 were waited for; matrix products, arithmetic and copies ran while one was open for 10% of the time, Pallas kernels for 0%

profile of v1, /device:TPU:0, one launch (start us, length us, event | category | flops | bytes accessed | tf_op | source)
XLA Modules:
  0.0 321.7 jit_solution(1051425155201373762)
XLA Ops:
  9.0 1.6 fusion.27
  15.1 48.8 %all-gather.7.cloned.1.call-done = bf16[768,2688]{1,0:T(8,128)(2,1)} async-done(((bf16[48,2688]{1,0:T(8,128)(2,1)}), bf16[768,2688]{1,0:T(8,128)(2,1)}) %all-gather.7.cloned.1.call-update) | async-done | bytes 4128784 | tf_op jit(solution)/shard_map/all_gather | solution.py:420
  63.9 2.4 slice.133.out_ref
  66.3 3.6 %slice.132.wcat_ref = bf16[768,1920]{1,0:T(8,128)(2,1)} slice(bf16[768,2688]{1,0:T(8,128)(2,1)} %all-gather.7.cloned.1.call-done), slice={[0:768], [0:1920]} | slice | bytes 5898240 | tf_op jit(solution)/shard_map/slice | solution.py:421
  69.9 21.3 %all-gather.9.cloned.1.call-done = bf16[1,1024,768]{2,1,0:T(8,128)(2,1)} async-done(((bf16[1,512,768]{2,1,0:T(8,128)(2,1)}), bf16[1,1024,768]{2,1,0:T(8,128)(2,1)}) %all-gather.9.cloned.1.call-update) | async-done | bytes 1572880 | tf_op jit(solution)/shard_map/all_gather | solution.py:426
  91.1 29.4 %all-gather.5.cloned.1.call-done.normed_ref = bf16[1024,768]{1,0:T(8,128)(2,1)} async-done(((bf16[512,768]{1,0:T(8,128)(2,1)}), bf16[1024,768]{1,0:T(8,128)(2,1)}) %all-gather.5.cloned.1.call-update) | async-done | bytes 1572880 | tf_op jit(solution)/shard_map/all_gather | solution.py:425
  120.5 23.4 %mixer_forward.1 = (f32[1024,1920]{1,0:T(8,128)}, f32[1024,1024]{1,0:T(8,128)}, f32[1024,768]{1,0:T(8,128)}, f32[1024,768]{1,0:T(8,128)}, f32[512,768]{1,0:T(8,1...) custom-call(bf16[1024,768]{1,0:T(8,128)(2,1)} %all-gather.5.cloned.1.call-done.normed_ref, bf16[1024,768]{1,0:T(8,128)(2,1)} %bitcast.145, ...), custom_call_target="tpu_custom_call" | custom-call | flops 5838471168 | bytes 26214400 | tf_op jit(solution)/shard_map/mixer_forward/pallas_call | solution.py:289
  146.8 12.0 %collective-permute-done = f32[2,1024]{0,1:T(8,128)S(1)} collective-permute-done((f32[2,1024]{0,1:T(8,128)S(1)}, f32[2,1024]{0,1:T(8,128)S(1)}, u32[]{:S(2)}, u32[]{:S(2)}) %collective-permute-start) | collective-permute-done | bytes 8224 | tf_op jit(solution)/shard_map/ppermute | solution.py:363
  159.9 44.0 %mixer_adjoint.1 = (bf16[1024,768]{1,0:T(8,128)(2,1)}, bf16[768,1920]{1,0:T(8,128)(2,1)}, f32[8,1024]{1,0:T(8,128)}, f32[8,128]{1,0:T(8,128)}, f32[8,768]{1,0:T(8,128)}) custom-call(bf16[1024,768]{1,0:T(8,128)(2,1)} %all-gather.5.cloned.1.call-done.normed_ref, f32[1024,1920]{1,0:T(8,128)} %get-tuple-element.29.raw_ref, ...), custom_call_target="tpu_custom_call" | custom-call | flops 10066329600 | bytes 26214400 | tf_op jit(solution)/shard_map/mixer_adjoint/pallas_call | solution.py:327
  205.4 2.5 slice.121
  208.0 1.5 slice.110
  209.5 1.4 slice_reduce_fusion
  211.6 3.9 %convolution_convert_fusion.1 = bf16[768,768]{0,1:T(8,128)(2,1)S(1)} fusion(bf16[1,1024,768]{2,1,0:T(8,128)(2,1)} %all-gather.9.cloned.1.call-done, f32[1024,768]{1,0:T(8,128)} %get-tuple-element.27, f32[768]{0:T(1024)S(1)} %copy-done.16, f32[1024]{0:T(1024)S(1)} %fusion.19), kind=kOutput, calls=%fused_computation.21 | convolution fusion | flops 1210908672 | bytes 5905408 | tf_op jit(solution)/shard_map/dot_general | solution.py:21
  215.8 1.7 copy-done.23
  217.5 2.8 convolution_convert_fusion
  221.8 1.6 collective-permute-start.2
  226.5 1.5 collective-permute-start.17
  229.0 1.5 collective-permute-start.13
  230.4 26.3 %collective-permute-done.2 = bf16[512,768]{1,0:T(8,128)(2,1)S(1)} collective-permute-done((bf16[512,768]{1,0:T(8,128)(2,1)S(1)}, bf16[512,768]{1,0:T(8,128)(2,1)S(1)}, u32[]{:S(2)}, u32[]{:S(2)}) %collective-permute-start.2) | collective-permute-done | bytes 786464 | tf_op jit(solution)/shard_map/ppermute | solution.py:363
  259.0 1.6 fusion.9
  260.7 1.5 collective-permute-start.8
  262.3 1.6 collective-permute-start.4
  264.6 1.6 collective-permute-start.9
  266.2 3.5 %fusion.6 = (f32[1,512,768]{2,1,0:T(8,128)}, bf16[1,512,768]{2,1,0:T(8,128)(2,1)}) fusion(bf16[512,768]{1,0:T(8,128)(2,1)S(1)} %copy-done.6, bf16[1,512,768]{2,1,0:T(8,128)(2,1)S(1)} %copy-done.4, bf16[1,512,768]{2,1,0:T(8,128)(2,1)S(1)} %copy-done, f32[512]{0:T(512)S(1)} %fusion.36, f32[768]{0:T(1024)S(1)} %copy-done.13, f32[512]{0:T(512)S(1)} %add_rsqrt_fusion, ...), kind=kLoop, calls=%fused_computation.14 | loop fusion | flops 5898240 | bytes 7085060 | tf_op jit(solution)/shard_map/broadcast_in_dim | solution.py:463
  269.8 4.2 %collective-permute-done.9 = f32[56,128]{1,0:T(8,128)S(1)} collective-permute-done((f32[56,128]{1,0:T(8,128)S(1)}, f32[56,128]{1,0:T(8,128)S(1)}, u32[]{:S(2)}, u32[]{:S(2)}) %collective-permute-start.9) | collective-permute-done | bytes 28704 | tf_op jit(solution)/shard_map/ppermute | solution.py:363
  274.0 2.4 collective-permute-start.10
  281.3 5.0 %collective-permute-done.18 = bf16[2,48,768]{2,1,0:T(8,128)(2,1)S(1)} collective-permute-done((bf16[2,48,768]{2,1,0:T(8,128)(2,1)S(1)}, bf16[2,48,768]{2,1,0:T(8,128)(2,1)S(1)}, u32[]{:S(2)}, u32[]{:S(2)}) %collective-permute-start.18) | collective-permute-done | bytes 147488 | tf_op jit(solution)/shard_map/ppermute | solution.py:363
  287.2 3.6 %collective-permute-done.19 = bf16[48,768]{1,0:T(8,128)(2,1)S(1)} collective-permute-done((bf16[48,768]{1,0:T(8,128)(2,1)S(1)}, bf16[48,768]{1,0:T(8,128)(2,1)S(1)}, u32[]{:S(2)}, u32[]{:S(2)}) %collective-permute-start.19) | collective-permute-done | bytes 73760 | tf_op jit(solution)/shard_map/ppermute | solution.py:363
  292.7 2.1 collective-permute-start.15
  294.8 8.8 %collective-permute-done.5 = bf16[2,48,1024]{2,1,0:T(8,128)(2,1)S(1)} collective-permute-done((bf16[2,48,1024]{2,1,0:T(8,128)(2,1)S(1)}, bf16[2,48,1024]{2,1,0:T(8,128)(2,1)S(1)}, u32[]{:S(2)}, u32[]{:S(2)}) %collective-permute-start.5) | collective-permute-done | bytes 196640 | tf_op jit(solution)/shard_map/ppermute | solution.py:363
  305.2 3.1 collective-permute-done.6
  310.7 2.0 collective-permute-done.11
  (157 shorter events, 34.8 us)
Async XLA Ops:
  7.2 4.4 %copy-start = (bf16[1,512,768]{2,1,0:T(8,128)(2,1)S(1)}, bf16[1,512,768]{2,1,0:T(8,128)(2,1)}, u32[]{:S(2)}) copy-start(bf16[1,512,768]{2,1,0:T(8,128)(2,1)} %param.15) | copy-start | bytes 2359300
  7.2 4.6 %copy-start.13 = (f32[768]{0:T(1024)S(1)}, f32[768]{0:T(1024)}, u32[]{:S(2)}) copy-start(f32[768]{0:T(1024)} %param.17) | copy-start | bytes 9220
  7.2 56.7 %all-gather.7.cloned.1.call-start = ((), (), s32[]{:S(2)}) async-start(), calls=%async_computation.1 | async-start | bytes 4386816 | tf_op jit(solution)/shard_map/all_gather | solution.py:420
  10.7 80.5 %all-gather.9.cloned.1.call-start = ((), (), s32[]{:S(2)}) async-start(), calls=%async_computation.2 | async-start | bytes 2359296 | tf_op jit(solution)/shard_map/all_gather | solution.py:426
  11.5 109.0 %all-gather.5.cloned.1.call-start = ((), (), s32[]{:S(2)}) async-start(), calls=%async_computation | async-start | bytes 2359296 | tf_op jit(solution)/shard_map/all_gather | solution.py:425
  143.9 14.9 %copy-start.11 = (f32[1024,128]{1,0:T(8,128)S(1)}, f32[1024,128]{1,0:T(8,128)}, u32[]{:S(2)}) copy-start(f32[1024,128]{1,0:T(8,128)} %get-tuple-element.28) | copy-start | bytes 1572868
  145.1 13.7 %collective-permute-start = (f32[2,1024]{0,1:T(8,128)S(1)}, f32[2,1024]{0,1:T(8,128)S(1)}, u32[]{:S(2)}, u32[]{:S(2)}) collective-permute-start(f32[2,1024]{0,1:T(8,128)S(1)} %slice_bitcast_fusion), channel_id=1, source_target_pairs={{0,1},{1,0},{2,3},{3,2},{4,5},{5,4},{6,7},{7,6},{8,9},{9,8},{10,11... | collective-permute-start | bytes 24584 | tf_op jit(solution)/shard_map/ppermute | solution.py:363
  215.7 9.8 %collective-permute-start.16 = (bf16[2,2,2,48,768]{4,3,2,0,1:T(8,128)(2,1)S(1)}, bf16[2,2,2,48,768]{4,3,2,0,1:T(8,128)(2,1)S(1)}, u32[]{:S(2)}, u32[]{:S(2)}) collective-permute-start(bf16[2,2,2,48,768]{4,3,2,0,1:T(8,128)(2,1)S(1)} %bitcast.133), channel_id=1, source_target_pairs={{0,2},{2,0},{4,6},{6,4},{8,10},{10,8},{12,14},{14,12},{16,18},{18,... | collective-permute-start | bytes 1769480 | tf_op jit(solution)/shard_map/ppermute | solution.py:363
  221.3 44.9 %collective-permute-start.1 = (bf16[512,768]{1,0:T(8,128)(2,1)}, bf16[512,768]{1,0:T(8,128)(2,1)}, u32[]{:S(2)}, u32[]{:S(2)}) collective-permute-start(bf16[512,768]{1,0:T(8,128)(2,1)} %constant_dynamic-slice_fusion.3), channel_id=1, source_target_pairs={{0,1},{1,0},{2,3},{3,2},{4,5},{5,4},{6,7},{7,6},{8,9},{9,8},{10,11... | collective-permute-start | bytes 2359304 | tf_op jit(solution)/shard_map/ppermute | solution.py:363
  221.8 34.9 %collective-permute-start.2 = (bf16[512,768]{1,0:T(8,128)(2,1)S(1)}, bf16[512,768]{1,0:T(8,128)(2,1)S(1)}, u32[]{:S(2)}, u32[]{:S(2)}) collective-permute-start(bf16[512,768]{1,0:T(8,128)(2,1)S(1)} %constant_dynamic-slice_fusion.2), channel_id=1, source_target_pairs={{0,1},{1,0},{2,3},{3,2},{4,5},{5,4},{6,7},{7,6},{8,9},{9,8},{10,11... | collective-permute-start | bytes 2359304 | tf_op jit(solution)/shard_map/ppermute | solution.py:363
  223.5 4.4 %collective-permute-start.12 = (bf16[2,2,2,48,896]{4,3,2,1,0:T(8,128)(2,1)S(1)}, bf16[2,2,2,48,896]{4,3,2,1,0:T(8,128)(2,1)S(1)}, u32[]{:S(2)}, u32[]{:S(2)}) collective-permute-start(bf16[2,2,2,48,896]{4,3,2,1,0:T(8,128)(2,1)S(1)} %dynamic-slice_bitcast_fusion.1), channel_id=1, source_target_pairs={{0,2},{2,0},{4,6},{6,4},{8,10},{10,8},{12,14},{14,12},{16,18},{18,... | collective-permute-start | bytes 2064392 | tf_op jit(solution)/shard_map/ppermute | solution.py:363
  224.9 34.1 %collective-permute-start.3 = (bf16[2,2,2,48,1024]{4,3,2,1,0:T(8,128)(2,1)S(1)}, bf16[2,2,2,48,1024]{4,3,2,1,0:T(8,128)(2,1)}, u32[]{:S(2)}, u32[]{:S(2)}) collective-permute-start(bf16[2,2,2,48,1024]{4,3,2,1,0:T(8,128)(2,1)S(1)} %dynamic-slice_bitcast_fusion), channel_id=1, source_target_pairs={{0,2},{2,0},{4,6},{6,4},{8,10},{10,8},{12,14},{14,12},{16,18},{18,... | collective-permute-start | bytes 2359304 | tf_op jit(solution)/shard_map/ppermute | solution.py:363
  226.5 50.0 %collective-permute-start.17 = (bf16[2,2,48,768]{3,2,1,0:T(8,128)(2,1)}, bf16[2,2,48,768]{3,2,1,0:T(8,128)(2,1)}, u32[]{:S(2)}, u32[]{:S(2)}) collective-permute-start(bf16[2,2,48,768]{3,2,1,0:T(8,128)(2,1)} %dynamic-slice_bitcast_fusion.4), channel_id=1, source_target_pairs={{0,8},{2,10},{4,12},{6,14},{8,0},{10,2},{12,4},{14,6},{16,24},{18,... | collective-permute-start | bytes 884744 | tf_op jit(solution)/shard_map/ppermute | solution.py:363
  228.2 29.9 %copy-start.7 = (bf16[2,2,2,48,896]{4,3,2,1,0:T(8,128)(2,1)}, bf16[2,2,2,48,896]{4,3,2,1,0:T(8,128)(2,1)S(1)}, u32[]{:S(2)}) copy-start(bf16[2,2,2,48,896]{4,3,2,1,0:T(8,128)(2,1)S(1)} %fusion.11) | copy-start | bytes 2064388
  229.0 58.0 %collective-permute-start.13 = (bf16[2,2,48,896]{3,2,1,0:T(8,128)(2,1)}, bf16[2,2,48,896]{3,2,1,0:T(8,128)(2,1)S(1)}, u32[]{:S(2)}, u32[]{:S(2)}) collective-permute-start(bf16[2,2,48,896]{3,2,1,0:T(8,128)(2,1)} %dynamic-slice_bitcast_fusion.3), channel_id=1, source_target_pairs={{0,4},{2,6},{4,0},{6,2},{8,12},{10,14},{12,8},{14,10},{16,20},{18,... | collective-permute-start | bytes 1032200 | tf_op jit(solution)/shard_map/ppermute | solution.py:363
  258.9 7.3 %copy-start.3 = (bf16[1024,768]{1,0:T(8,128)(2,1)S(1)}, bf16[1024,768]{1,0:T(8,128)(2,1)}, u32[]{:S(2)}) copy-start(bf16[1024,768]{1,0:T(8,128)(2,1)} %get-tuple-element.34) | copy-start | bytes 4718596
  258.9 7.3 %copy-start.4 = (bf16[1,512,768]{2,1,0:T(8,128)(2,1)S(1)}, bf16[1,512,768]{2,1,0:T(8,128)(2,1)}, u32[]{:S(2)}) copy-start(bf16[1,512,768]{2,1,0:T(8,128)(2,1)} %param.16) | copy-start | bytes 2359300
  258.9 7.3 %copy-start.6 = (bf16[512,768]{1,0:T(8,128)(2,1)S(1)}, bf16[512,768]{1,0:T(8,128)(2,1)}, u32[]{:S(2)}) copy-start(bf16[512,768]{1,0:T(8,128)(2,1)} %copy-done.5) | copy-start | bytes 2359300
  259.0 1.7 collective-permute-start.7
  260.7 3.9 %collective-permute-start.8 = (f32[56,128]{1,0:T(8,128)S(1)}, f32[56,128]{1,0:T(8,128)S(1)}, u32[]{:S(2)}, u32[]{:S(2)}) collective-permute-start(f32[56,128]{1,0:T(8,128)S(1)} %fusion.38), channel_id=1, source_target_pairs={{0,4},{2,6},{4,0},{6,2},{8,12},{10,14},{12,8},{14,10},{16,20},{18,... | collective-permute-start | bytes 86024 | tf_op jit(solution)/shard_map/ppermute | solution.py:363
  262.3 29.2 %collective-permute-start.4 = (bf16[2,2,48,1024]{3,2,1,0:T(8,128)(2,1)S(1)}, bf16[2,2,48,1024]{3,2,1,0:T(8,128)(2,1)S(1)}, u32[]{:S(2)}, u32[]{:S(2)}) collective-permute-start(bf16[2,2,48,1024]{3,2,1,0:T(8,128)(2,1)S(1)} %dynamic-slice_bitcast_fusion.2), channel_id=1, source_target_pairs={{0,8},{2,10},{4,12},{6,14},{8,0},{10,2},{12,4},{14,6},{16,24},{18,... | collective-permute-start | bytes 1179656 | tf_op jit(solution)/shard_map/ppermute | solution.py:363
  264.6 11.8 %copy-start.10 = (bf16[2,2,2,48,768]{4,3,2,0,1:T(8,128)(2,1)S(1)}, bf16[2,2,2,48,768]{4,3,2,0,1:T(8,128)(2,1)}, u32[]{:S(2)}) copy-start(bf16[2,2,2,48,768]{4,3,2,0,1:T(8,128)(2,1)} %copy-done.9) | copy-start | bytes 1769476
  264.6 9.4 %collective-permute-start.9 = (f32[56,128]{1,0:T(8,128)S(1)}, f32[56,128]{1,0:T(8,128)S(1)}, u32[]{:S(2)}, u32[]{:S(2)}) collective-permute-start(f32[56,128]{1,0:T(8,128)S(1)} %fusion.42), channel_id=1, source_target_pairs={{0,8},{2,10},{4,12},{6,14},{8,0},{10,2},{12,4},{14,6},{16,24},{18,... | collective-permute-start | bytes 86024 | tf_op jit(solution)/shard_map/ppermute | solution.py:363
  269.8 17.2 %copy-start.8 = (bf16[2,2,2,48,896]{4,3,2,1,0:T(8,128)(2,1)S(1)}, bf16[2,2,2,48,896]{4,3,2,1,0:T(8,128)(2,1)}, u32[]{:S(2)}) copy-start(bf16[2,2,2,48,896]{4,3,2,1,0:T(8,128)(2,1)} %copy-done.7) | copy-start | bytes 2064388
  274.0 4.8 %collective-permute-start.10 = (f32[56,128]{1,0:T(8,128)S(1)}, f32[56,128]{1,0:T(8,128)S(1)}, u32[]{:S(2)}, u32[]{:S(2)}) collective-permute-start(f32[56,128]{1,0:T(8,128)S(1)} %add.189), channel_id=1, source_target_pairs={{0,16},{2,18},{4,20},{6,22},{8,24},{10,26},{12,28},{14,30},{16,0},... | collective-permute-start | bytes 86024 | tf_op jit(solution)/shard_map/ppermute | solution.py:363
  277.5 8.8 %collective-permute-start.18 = (bf16[2,48,768]{2,1,0:T(8,128)(2,1)S(1)}, bf16[2,48,768]{2,1,0:T(8,128)(2,1)S(1)}, u32[]{:S(2)}, u32[]{:S(2)}) collective-permute-start(bf16[2,48,768]{2,1,0:T(8,128)(2,1)S(1)} %dynamic-slice_bitcast_fusion.7), channel_id=1, source_target_pairs={{0,16},{2,18},{4,20},{6,22},{8,24},{10,26},{12,28},{14,30},{16,0},... | collective-permute-start | bytes 442376 | tf_op jit(solution)/shard_map/ppermute | solution.py:363
  286.4 4.4 %collective-permute-start.19 = (bf16[48,768]{1,0:T(8,128)(2,1)S(1)}, bf16[48,768]{1,0:T(8,128)(2,1)S(1)}, u32[]{:S(2)}, u32[]{:S(2)}) collective-permute-start(bf16[48,768]{1,0:T(8,128)(2,1)S(1)} %dynamic-slice_bitcast_fusion.10), channel_id=1, source_target_pairs={{0,4},{2,6},{4,0},{6,2},{8,12},{10,14},{12,8},{14,10},{16,20},{18,... | collective-permute-start | bytes 221192 | tf_op jit(solution)/shard_map/ppermute | solution.py:363
  287.1 5.5 %collective-permute-start.14 = (bf16[2,48,896]{2,1,0:T(8,128)(2,1)S(1)}, bf16[2,48,896]{2,1,0:T(8,128)(2,1)S(1)}, u32[]{:S(2)}, u32[]{:S(2)}) collective-permute-start(bf16[2,48,896]{2,1,0:T(8,128)(2,1)S(1)} %dynamic-slice_bitcast_fusion.6), channel_id=1, source_target_pairs={{0,8},{2,10},{4,12},{6,14},{8,0},{10,2},{12,4},{14,6},{16,24},{18,... | collective-permute-start | bytes 516104 | tf_op jit(solution)/shard_map/ppermute | solution.py:363
  291.6 12.0 %collective-permute-start.5 = (bf16[2,48,1024]{2,1,0:T(8,128)(2,1)S(1)}, bf16[2,48,1024]{2,1,0:T(8,128)(2,1)S(1)}, u32[]{:S(2)}, u32[]{:S(2)}) collective-permute-start(bf16[2,48,1024]{2,1,0:T(8,128)(2,1)S(1)} %dynamic-slice_bitcast_fusion.5), channel_id=1, source_target_pairs={{0,16},{2,18},{4,20},{6,22},{8,24},{10,26},{12,28},{14,30},{16,0},... | collective-permute-start | bytes 589832 | tf_op jit(solution)/shard_map/ppermute | solution.py:363
  292.7 12.5 %collective-permute-start.15 = (bf16[48,896]{1,0:T(8,128)(2,1)S(1)}, bf16[48,896]{1,0:T(8,128)(2,1)S(1)}, u32[]{:S(2)}, u32[]{:S(2)}) collective-permute-start(bf16[48,896]{1,0:T(8,128)(2,1)S(1)} %dynamic-slice_bitcast_fusion.9), channel_id=1, source_target_pairs={{0,16},{2,18},{4,20},{6,22},{8,24},{10,26},{12,28},{14,30},{16,0},... | collective-permute-start | bytes 258056 | tf_op jit(solution)/shard_map/ppermute | solution.py:363
  303.7 4.7 %collective-permute-start.6 = (bf16[48,1024]{1,0:T(8,128)(2,1)S(1)}, bf16[48,1024]{1,0:T(8,128)(2,1)S(1)}, u32[]{:S(2)}, u32[]{:S(2)}) collective-permute-start(bf16[48,1024]{1,0:T(8,128)(2,1)S(1)} %dynamic-slice_bitcast_fusion.8), channel_id=1, source_target_pairs={{0,4},{2,6},{4,0},{6,2},{8,12},{10,14},{12,8},{14,10},{16,20},{18,... | collective-permute-start | bytes 294920 | tf_op jit(solution)/shard_map/ppermute | solution.py:363
  308.5 4.2 %collective-permute-start.11 = (f32[112,128]{1,0:T(8,128)S(1)}, f32[112,128]{1,0:T(8,128)S(1)}, u32[]{:S(2)}, u32[]{:S(2)}) collective-permute-start(f32[112,128]{1,0:T(8,128)S(1)} %maximum_bitcast_fusion), channel_id=1, source_target_pairs={{0,1},{1,0},{2,3},{3,2},{4,5},{5,4},{6,7},{7,6},{8,9},{9,8},{10,11... | collective-permute-start | bytes 172040 | tf_op jit(solution)/shard_map/ppermute | solution.py:363
  (15 other events, 33.3 us)
Sparse Core Ops, SparseCore 0:
  10.9 52.9 all-gather.6
  65.4 25.6 all-gather.8
  93.3 27.2 all-gather.4

commit v2 on v1

--- a/solution.py
+++ b/solution.py
@@ -54,8 +54,8 @@
 
 
 def forward_kernel(
-    normed_ref, cot_ref, wcat_ref, out_ref, cw_ref, hp_ref, ch_ref,
-    raw_ref, conv_ref, scanned_ref, gated_ref, state_out_ref, dng_ref, stats_ref,
+    normed_ref, wcat_ref, cw_ref, hp_ref, ch_ref,
+    raw_ref, conv_ref, scanned_ref, gated_ref, state_out_ref,
     buf, state, fresh_in,
 ):
     at = pl.program_id(0)
@@ -116,18 +116,12 @@
     gate_z = raw_ref[:, 0:width]
     gated = scanned_ref[...] * (gate_z * sigmoid(gate_z))
     gated_ref[...] = gated
-    dng = mm(cot_ref[...], out_ref[...])
-    dng_ref[...] = dng
-    squares = jnp.sum(gated * gated, axis=1, keepdims=True)
-    cross = jnp.sum(dng * ch_ref[1:2, :] * gated, axis=1, keepdims=True)
-    lane = lax.broadcasted_iota(jnp.int32, (span, PAD), 1)
-    stats_ref[...] = jnp.where(lane == 0, squares, jnp.where(lane == 1, cross, 0.0))
 
 
 def backward_kernel(
     normed_ref, raw_ref, conv_ref, scanned_ref, state_ref, dng_ref, stats_ref,
     wcat_ref, cw_ref, hp_ref, ch_ref, sum_ref,
-    partial_ref, grads_ref, gcw_ref, ghp_ref, gch_ref,
+    partial_ref, grads_a_ref, grads_b_ref, gcw_ref, ghp_ref, gch_ref,
     adjoint, buf, acc, dye, ut, dz, prod, score_sum,
 ):
     at = pl.program_id(0)
@@ -148,7 +142,7 @@
     def _():
         buf[span : span + 8, :] = buf[0:8, :]
 
-    stats = stats_ref[...]
+    stats = jnp.concatenate([stats_ref[...], jnp.zeros((PAD - 8, span), F32)], axis=0).T
     scale = lax.rsqrt(stats[:, 0:1] / INNER + EPSILON)
     pull = scale * scale * scale * stats[:, 1:2] / INNER
     gate_z = raw_ref[:, 0:width]
@@ -274,10 +268,12 @@
 
     @pl.when(at == pl.num_programs(0) - 1)
     def _():
-        grads_ref[...] = acc[...].astype(BF16)
-
-
-def forward_part(normed, cot, wcat, out_t, cw, hp, ch):
+        cut = grads_a_ref.shape[1]
+        grads_a_ref[...] = acc[:, :cut].astype(BF16)
+        grads_b_ref[...] = acc[:, cut:].astype(BF16)
+
+
+def forward_part(normed, wcat, cw, hp, ch):
     length, model = normed.shape
     width = ch.shape[1]
     both = width + 2 * NSTATE
@@ -289,14 +285,14 @@
     return pl.pallas_call(
         forward_kernel,
         grid=(blocks,),
-        in_specs=[row(model), row(model), whole(wcat), whole(out_t), whole(cw), whole(hp), whole(ch)],
+        in_specs=[row(model), whole(wcat), whole(cw), whole(hp), whole(ch)],
         out_specs=[
             row(cat), row(both), row(width), row(width),
-            pl.BlockSpec((NSTATE, width), lambda i: (i, 0)), row(width), row(PAD),
+            pl.BlockSpec((NSTATE, width), lambda i: (i, 0)),
         ],
         out_shape=[
             shape(length, cat), shape(length, both), shape(length, width), shape(length, width),
-            shape(blocks * NSTATE, width), shape(length, width), shape(length, PAD),
+            shape(blocks * NSTATE, width),
         ],
         scratch_shapes=[
             pltpu.VMEM((SPAN + 8, both), F32),
@@ -309,7 +305,7 @@
             bytes_accessed=25 * 2**20, transcendentals=length * width * 6,
         ),
         name="mixer_forward",
-    )(normed, cot, wcat, out_t, cw, hp, ch)
+    )(normed, wcat, cw, hp, ch)
 
 
 def backward_part(normed, raw, conv, scanned, states, dng, stats, wcat, cw, hp, ch):
@@ -318,6 +314,7 @@
     both = width + 2 * NSTATE
     cat = wcat.shape[1]
     blocks = length // SPAN
+    cut = cat // 256 * 128
     summer = (
         lax.broadcasted_iota(jnp.int32, (width, PAD), 0) // 64
         == lax.broadcasted_iota(jnp.int32, (width, PAD), 1)
@@ -329,13 +326,16 @@
         grid=(blocks,),
         in_specs=[
             row(model), row(cat), row(both), row(width),
-            pl.BlockSpec((NSTATE, width), lambda i: (blocks - 1 - i, 0)), row(width), row(PAD),
+            pl.BlockSpec((NSTATE, width), lambda i: (blocks - 1 - i, 0)), row(width), pl.BlockSpec((8, SPAN), lambda i: (0, blocks - 1 - i)),
             whole(wcat), whole(cw), whole(hp), whole(ch), whole(summer),
         ],
-        out_specs=[row(model), whole(wcat), whole(cw), whole(hp), whole(ch)],
+        out_specs=[
+            row(model), pl.BlockSpec((model, cut), lambda i: (0, 0)),
+            pl.BlockSpec((model, cat - cut), lambda i: (0, 0)), whole(cw), whole(hp), whole(ch)],
         out_shape=[
             jax.ShapeDtypeStruct((length, model), BF16),
-            jax.ShapeDtypeStruct((model, cat), BF16),
+            jax.ShapeDtypeStruct((model, cut), BF16),
+            jax.ShapeDtypeStruct((model, cat - cut), BF16),
             jax.ShapeDtypeStruct(cw.shape, F32),
             jax.ShapeDtypeStruct(hp.shape, F32),
             jax.ShapeDtypeStruct(ch.shape, F32),
@@ -363,13 +363,10 @@
     return lax.ppermute(values, axis, [(i, i ^ bit) for i in range(size)])
 
 
-def scatter_sum(values, size, order):
+def scatter_steps(held, size, order, start, stop):
     me = lax.axis_index("dp")
-    bits = size.bit_length() - 1
-    rows = values.shape[0] // size
-    held = values.reshape((2,) * bits + (rows, values.shape[1]))
-    left = list(range(bits - 1, -1, -1))
-    for bit in order:
+    left = [bit for bit in range(size.bit_length() - 2, -1, -1) if bit not in order[:start]]
+    for bit in order[start:stop]:
         axis = left.index(bit)
         mine = (me >> bit) & 1
         keep = lax.dynamic_index_in_dim(held, mine, axis, keepdims=False)
@@ -380,6 +377,16 @@
     return held
 
 
+def scatter_sum(values, size, order, stop=None):
+    rows = values.shape[0] // size
+    held = values.reshape((2,) * len(order) + (rows, values.shape[1]))
+    return scatter_steps(held, size, order, 0, stop)
+
+
+def scatter_rest(held, size, order, start):
+    return scatter_steps(held, size, order, start, None)
+
+
 def whole_sum(values, axis, size):
     bit = 1
     while bit < size:
@@ -396,6 +403,16 @@
     keep = lax.dynamic_slice_in_dim(values, me * half, half, 0)
     send = lax.dynamic_slice_in_dim(values, (1 - me) * half, half, 0)
     return keep.astype(F32) + swap(send, 1, "tensor", 2).astype(F32)
+
+
+def token_gather(values, size):
+    if size != 2:
+        return lax.all_gather(values, "tensor", axis=0, tiled=True)
+    got = swap(values, 1, "tensor", 2)
+    is_first = lax.axis_index("tensor") == 0
+    return jnp.concatenate(
+        [jnp.where(is_first, values, got), jnp.where(is_first, got, values)], axis=0
+    )
 
 
 def on_device(
@@ -413,17 +430,17 @@
             gate_inner_projection.reshape(share, 2 * width),
             proj_bc,
             jnp.pad(proj_dt, ((0, 0), (0, PAD - heads))),
-            proj_out.T,
         ],
         axis=1,
     )
-    weights = lax.all_gather(packed, "dp", axis=0, tiled=True)
-    wcat, out_t = weights[:, :cat], weights[:, cat:]
+    wcat = lax.all_gather(packed, "dp", axis=0, tiled=True)
     token_rows = tokens[0].astype(F32)
     inv_rms = lax.rsqrt(jnp.mean(token_rows * token_rows, axis=-1, keepdims=True) + EPSILON)
     local_normed = (token_rows * inv_rms * norm_in).astype(BF16)
-    normed = lax.all_gather(local_normed, "tensor", axis=0, tiled=True)
-    cot = lax.all_gather(cotangent[0], "tensor", axis=0, tiled=True)
+    normed = token_gather(local_normed, tp)
+    cot = token_gather(cotangent[0], tp)
+    out_rows, wcat, normed = lax.optimization_barrier((proj_out.T, wcat, normed))
+    out_t = lax.all_gather(out_rows, "dp", axis=0, tiled=True)
     cw = jnp.pad(
         jnp.concatenate(
             [
@@ -436,26 +453,34 @@
     )
     hp = jnp.pad(jnp.stack([step_bias, log_decay]), ((0, 6), (0, PAD - heads)))
     ch = jnp.pad(jnp.stack([jnp.repeat(skip_gain, width // heads), norm_gate]), ((0, 6), (0, 0)))
-    raw, conv, scanned, gated, states, dng, stats = forward_part(
-        normed, cot, wcat, out_t, cw, hp, ch
-    )
-    stats = jnp.pad(
-        whole_sum(stats[:, :2].T, "tensor", tp).T, ((0, 0), (0, PAD - 2))
-    )
-    scale = lax.rsqrt(stats[:, 0:1] / INNER + EPSILON)
+    raw, conv, scanned, gated, states = forward_part(normed, wcat, cw, hp, ch)
+    dng = mm(cot, out_t)
+    stats = jnp.stack(
+        [jnp.sum(gated * gated, axis=1), jnp.sum(dng * norm_gate * gated, axis=1)]
+    )
+    stats = jnp.pad(stats, ((0, 6), (0, 0)))
+    stats = whole_sum(stats, "tensor", tp)
+    scale = lax.rsqrt(stats[0][:, None] / INNER + EPSILON)
     gate_normed = (gated * scale * norm_gate).astype(BF16)
-    branch = token_scatter(mm(gate_normed, out_t, 1, 1).astype(BF16), tp)
-    block_out = (token_rows + branch).astype(BF16)[None]
+    branch_part = mm(gate_normed, out_t, 1, 1).astype(BF16)
     bits = dp.bit_length() - 1
     order = tuple(range(bits))
     other = (0,) + tuple(range(2, bits)) + (1,)
-    grad_out = scatter_sum(mm(cot, gate_normed, 0, 0).astype(BF16), dp, other)
-    partial, grads, gcw, ghp, gch = backward_part(
+    out_part = mm(cot, gate_normed, 0, 0).astype(BF16)
+    branch_part, out_part, stats = lax.optimization_barrier((branch_part, out_part, stats))
+    branch = token_scatter(branch_part, tp)
+    out_first = (1,) + tuple(b for b in order if b != 1)
+    grad_out = scatter_sum(out_part, dp, out_first, 1)
+    partial, grads_a, grads_b, gcw, ghp, gch = backward_part(
         normed, raw, conv, scanned, states, dng, stats, wcat, cw, hp, ch
     )
-    cut = cat // 256 * 128
+    branch, grad_out, partial, grads_a, grads_b = lax.optimization_barrier(
+        (branch, grad_out, partial, grads_a, grads_b)
+    )
+    block_out = (token_rows + branch).astype(BF16)[None]
+    grad_out = scatter_rest(grad_out, dp, out_first, 1)
     grads = jnp.concatenate(
-        [scatter_sum(grads[:, :cut], dp, order), scatter_sum(grads[:, cut:], dp, other)], axis=1
+        [scatter_sum(grads_a, dp, order), scatter_sum(grads_b, dp, other)], axis=1
     )
     d_rows = token_scatter(partial, tp)
     gained = norm_in * d_rows

time: 322 us -> 250 us (0.78)
  waiting for transfers between devices: 168 us -> 92.2 us
  local copies, waits for them, and re-layouts: 30.3 us -> 19.5 us
  starting transfers between devices: 18.7 us -> 27.9 us
  matrix products: 6.76 us -> 10.5 us
  other arithmetic: 16 us -> 19.3 us
    all_gather x3 -> x2, waiting for transfers between devices: 99.5 us -> 23.1 us  [the longest x1 23.1 us: on_device(): wcat = lax.all_gather(packed, 'dp', axis=0, tiled=True)]
    slice x4 -> x0, local copies, waits for them, and re-layouts: 10 us -> none  [the longest x2 5.99 us: on_device(): wcat, out_t = (weights[:, :cat], weights[:, cat:])]
    ppermute x20 -> x22, starting transfers between devices: 18.6 us -> 27.8 us  [swap(): return lax.ppermute(values, axis, [(i, i ^ bit) for i in range(size)])]
    dot_general x2 -> x3, matrix products: 6.76 us -> 10.5 us  [mm(): lax.dot_general(left, right, (((left_dim,), (right_dim,)), ((), ())), pre...]
    ppermute x20 -> x22, waiting for transfers between devices: 67.8 us -> 69 us  [swap(): return lax.ppermute(values, axis, [(i, i ^ bit) for i in range(size)])]
  transfers between devices with their start and end apart: 23 -> 24, of which waited for: 15 -> 14; matrix products, arithmetic and copies ran while one was open for 10% -> 12% of each run, Pallas kernels for 0% -> 26%
where the time goes in v2:
time: 250 us
  waiting for transfers between devices  92.2 us (37%)
  Pallas kernels  65.5 us (26%)
  starting transfers between devices  27.9 us (11%)
  local copies, waits for them, and re-layouts  19.5 us (8%)
  other arithmetic  19.3 us (8%)
  between operations  14.7 us (6%)
  matrix products  10.5 us (4%)
    ppermute x22, waiting for transfers between devices, swap(): return lax.ppermute(values, axis, [(i, i ^ bit) for i in range(size)])  69 us
    pallas_call x1, Pallas kernels, backward_part(): pl.pallas_call(backward_kernel, grid=(blocks,), in_specs=[row(model), row...  44 us
    ppermute x22, starting transfers between devices, swap(): return lax.ppermute(values, axis, [(i, i ^ bit) for i in range(size)])  27.8 us
    all_gather x1, waiting for transfers between devices, on_device(): wcat = lax.all_gather(packed, 'dp', axis=0, tiled=True)  23.1 us
    pallas_call x1, Pallas kernels, forward_part(): pl.pallas_call(forward_kernel, grid=(blocks,), in_specs=[row(model), whol...  21.5 us
    dot_general x3, matrix products, mm(): lax.dot_general(left, right, (((left_dim,), (right_dim,)), ((), ())), pre...  10.5 us
  transfers between devices with their start and end apart: 24, of which 14 were waited for; matrix products, arithmetic and copies ran while one was open for 12% of the time, Pallas kernels for 26%

profile of v2, /device:TPU:0, one launch (start us, length us, event | category | flops | bytes accessed | tf_op | source)
XLA Modules:
  0.0 249.7 jit_solution(14435255876909361562)
XLA Ops:
  9.0 1.4 fusion.24
  12.7 3.0 %collective-permute-start = (bf16[512,768]{1,0:T(8,128)(2,1)S(1)}, bf16[512,768]{1,0:T(8,128)(2,1)S(1)}, u32[]{:S(2)}, u32[]{:S(2)}) collective-permute-start(bf16[512,768]{1,0:T(8,128)(2,1)S(1)} %fusion.2), channel_id=1, source_target_pairs={{0,1},{1,0},{2,3},{3,2},{4,5},{5,4},{6,7},{7,6},{8,9},{9,8},{10,11... | collective-permute-start | bytes 2359304 | tf_op jit(solution)/shard_map/ppermute | solution.py:363
  15.7 17.5 %collective-permute-done = bf16[512,768]{1,0:T(8,128)(2,1)S(1)} collective-permute-done((bf16[512,768]{1,0:T(8,128)(2,1)S(1)}, bf16[512,768]{1,0:T(8,128)(2,1)S(1)}, u32[]{:S(2)}, u32[]{:S(2)}) %collective-permute-start) | collective-permute-done | bytes 786464 | tf_op jit(solution)/shard_map/ppermute | solution.py:363
  35.1 23.1 %all-gather.3.cloned.1.call-done.wcat_ref = bf16[768,1920]{1,0:T(8,128)(2,1)} async-done(((bf16[48,1920]{1,0:T(8,128)(2,1)}), bf16[768,1920]{1,0:T(8,128)(2,1)}) %all-gather.3.cloned.1.call-update) | async-done | bytes 2949136 | tf_op jit(solution)/shard_map/all_gather | solution.py:436
  58.3 1.5 collective-permute-start.1
  61.9 16.3 %collective-permute-done.1 = bf16[512,768]{1,0:T(8,128)(2,1)} collective-permute-done((bf16[512,768]{1,0:T(8,128)(2,1)S(1)}, bf16[512,768]{1,0:T(8,128)(2,1)}, u32[]{:S(2)}, u32[]{:S(2)}) %collective-permute-start.1) | collective-permute-done | bytes 786464 | tf_op jit(solution)/shard_map/ppermute | solution.py:363
  79.4 21.5 %mixer_forward.1 = (f32[1024,1920]{1,0:T(8,128)}, f32[1024,1024]{1,0:T(8,128)}, f32[1024,768]{1,0:T(8,128)}, f32[1024,768]{1,0:T(8,128)}, f32[512,768]{1,0:T(8,128)}) custom-call(bf16[1024,768]{1,0:T(8,128)(2,1)} %pad_maximum_fusion.normed_ref, bf16[768,1920]{1,0:T(8,128)(2,1)} %all-gather.3.cloned.1.call-done.wcat_ref, ...), custom_call_target="tpu_custom_call" | custom-call | flops 5838471168 | bytes 26214400 | tf_op jit(solution)/shard_map/mixer_forward/pallas_call | solution.py:285
  100.9 5.4 %multiply_reduce_fusion.1 = (f32[1024]{0:T(1024)S(1)}, f32[1024]{0:T(1024)S(1)}, f32[1024,768]{1,0:T(8,128)}) fusion(f32[1024,768]{1,0:T(8,128)} %get-tuple-element.39, f32[768]{0:T(1024)S(1)} %copy-done.18, bf16[768,768]{1,0:T(8,128)(2,1)} %all-gather.5.cloned.1.call-done, bf16[512,768]{1,0:T(8,128)(2,1)S(1)} %get-tuple-element.81, ...), kind=kOutput, calls=%fused_computation.8 | convolution fusion | flops 1215035392 | bytes 9055232 | tf_op jit(solution)/shard_map/dot_general | solution.py:21
  106.3 1.5 collective-permute-start.2
  110.3 3.7 %convolution_convert_fusion.1 = bf16[768,768]{1,0:T(8,128)(2,1)S(1)} fusion(bf16[512,768]{1,0:T(8,128)(2,1)S(1)} %get-tuple-element.81, bf16[512,768]{1,0:T(8,128)(2,1)S(1)} %get-tuple-element.80, f32[1024,768]{1,0:T(8,128)} %get-tuple-element.39, f32[1024]{0:T(1024)S(1)} %bitcast.145, f32[768]{0:T(1024)S(1)} %copy-done.18), kind=kOutput, calls=%fused_computation.25 | convolution fusion | flops 1214054400 | bytes 5905408 | tf_op jit(solution)/shard_map/dot_general | solution.py:21
  114.0 1.5 convolution_convert_fusion
  115.6 1.5 collective-permute-start.3
  117.9 44.0 %mixer_adjoint.1 = (bf16[1024,768]{1,0:T(8,128)(2,1)}, bf16[768,896]{1,0:T(8,128)(2,1)}, bf16[768,1024]{1,0:T(8,128)(2,1)}, f32[8,1024]{1,0:T(8,128)}, f32[8,128]{1,0:T(8,128)}, /*index=5*/f32[8,768]{1,0:T(8,128)}) custom-call(bf16[1024,768]{1,0:T(8,128)(2,1)} %pad_maximum_fusion.normed_ref, f32[1024,1920]{1,0:T(8,128)} %get-tuple-element.43.raw_ref, ...), custom_call_target="tpu_custom_call" | custom-call | flops 10066329600 | bytes 26214400 | tf_op jit(solution)/shard_map/mixer_adjoint/pallas_call | solution.py:324
  164.7 1.5 convert_add_fusion.3
  171.9 1.5 collective-permute-start.20
  175.7 2.5 %collective-permute-done.20 = bf16[2,48,768]{2,1,0:T(8,128)(2,1)S(1)} collective-permute-done((bf16[2,48,768]{2,1,0:T(8,128)(2,1)S(1)}, bf16[2,48,768]{2,1,0:T(8,128)(2,1)S(1)}, u32[]{:S(2)}, u32[]{:S(2)}) %collective-permute-start.20) | collective-permute-done | bytes 147488 | tf_op jit(solution)/shard_map/ppermute | solution.py:363
  178.3 1.7 collective-permute-start.21
  180.2 4.7 %collective-permute-done.21 = bf16[48,768]{1,0:T(8,128)(2,1)S(1)} collective-permute-done((bf16[48,768]{1,0:T(8,128)(2,1)S(1)}, bf16[48,768]{1,0:T(8,128)(2,1)S(1)}, u32[]{:S(2)}, u32[]{:S(2)}) %collective-permute-start.21) | collective-permute-done | bytes 73760 | tf_op jit(solution)/shard_map/ppermute | solution.py:363
  186.7 1.5 collective-permute-start.16
  188.2 6.2 %collective-permute-done.5 = bf16[512,768]{1,0:T(8,128)(2,1)S(1)} collective-permute-done((bf16[512,768]{1,0:T(8,128)(2,1)S(1)}, bf16[512,768]{1,0:T(8,128)(2,1)S(1)}, u32[]{:S(2)}, u32[]{:S(2)}) %collective-permute-start.5) | collective-permute-done | bytes 786464 | tf_op jit(solution)/shard_map/ppermute | solution.py:363
  195.5 1.8 fusion.9
  197.4 1.5 collective-permute-start.11
  198.9 2.4 collective-permute-done.11
  206.2 2.1 fusion.6
  208.3 4.2 %collective-permute-done.13 = f32[56,128]{1,0:T(8,128)S(1)} collective-permute-done((f32[56,128]{1,0:T(8,128)S(1)}, f32[56,128]{1,0:T(8,128)S(1)}, u32[]{:S(2)}, u32[]{:S(2)}) %collective-permute-start.13) | collective-permute-done | bytes 28704 | tf_op jit(solution)/shard_map/ppermute | solution.py:363
  216.2 2.8 %collective-permute-start.17 = (bf16[2,48,896]{2,1,0:T(8,128)(2,1)S(1)}, bf16[2,48,896]{2,1,0:T(8,128)(2,1)S(1)}, u32[]{:S(2)}, u32[]{:S(2)}) collective-permute-start(bf16[2,48,896]{2,1,0:T(8,128)(2,1)S(1)} %dynamic-slice_bitcast_fusion.6), channel_id=1, source_target_pairs={{0,8},{2,10},{4,12},{6,14},{8,0},{10,2},{12,4},{14,6},{16,24},{18,... | collective-permute-start | bytes 516104 | tf_op jit(solution)/shard_map/ppermute | solution.py:363
  219.9 3.6 %collective-permute-done.17 = bf16[2,48,896]{2,1,0:T(8,128)(2,1)S(1)} collective-permute-done((bf16[2,48,896]{2,1,0:T(8,128)(2,1)S(1)}, bf16[2,48,896]{2,1,0:T(8,128)(2,1)S(1)}, u32[]{:S(2)}, u32[]{:S(2)}) %collective-permute-start.17) | collective-permute-done | bytes 172064 | tf_op jit(solution)/shard_map/ppermute | solution.py:363
  223.6 3.3 %collective-permute-start.18 = (bf16[48,896]{1,0:T(8,128)(2,1)S(1)}, bf16[48,896]{1,0:T(8,128)(2,1)S(1)}, u32[]{:S(2)}, u32[]{:S(2)}) collective-permute-start(bf16[48,896]{1,0:T(8,128)(2,1)S(1)} %dynamic-slice_bitcast_fusion.9), channel_id=1, source_target_pairs={{0,16},{2,18},{4,20},{6,22},{8,24},{10,26},{12,28},{14,30},{16,0},... | collective-permute-start | bytes 258056 | tf_op jit(solution)/shard_map/ppermute | solution.py:363
  226.9 4.5 %collective-permute-done.8 = bf16[2,48,1024]{2,1,0:T(8,128)(2,1)S(1)} collective-permute-done((bf16[2,48,1024]{2,1,0:T(8,128)(2,1)S(1)}, bf16[2,48,1024]{2,1,0:T(8,128)(2,1)S(1)}, u32[]{:S(2)}, u32[]{:S(2)}) %collective-permute-start.8) | collective-permute-done | bytes 196640 | tf_op jit(solution)/shard_map/ppermute | solution.py:363
  231.4 1.5 collective-permute-start.9
  233.0 3.1 %collective-permute-done.9 = bf16[48,1024]{1,0:T(8,128)(2,1)S(1)} collective-permute-done((bf16[48,1024]{1,0:T(8,128)(2,1)S(1)}, bf16[48,1024]{1,0:T(8,128)(2,1)S(1)}, u32[]{:S(2)}, u32[]{:S(2)}) %collective-permute-start.9) | collective-permute-done | bytes 98336 | tf_op jit(solution)/shard_map/ppermute | solution.py:363
  238.8 1.6 collective-permute-done.14
  (170 shorter events, 41.0 us)
Async XLA Ops:
  7.2 51.0 %all-gather.3.cloned.1.call-start = ((), (), s32[]{:S(2)}) async-start(), calls=%async_computation | async-start | bytes 3133440 | tf_op jit(solution)/shard_map/all_gather | solution.py:436
  10.5 90.4 %all-gather.5.cloned.1.call-start = ((), (), s32[]{:S(2)}) async-start(), calls=%async_computation.1 | async-start | bytes 1253376 | tf_op jit(solution)/shard_map/all_gather | solution.py:443
  12.7 20.5 %collective-permute-start = (bf16[512,768]{1,0:T(8,128)(2,1)S(1)}, bf16[512,768]{1,0:T(8,128)(2,1)S(1)}, u32[]{:S(2)}, u32[]{:S(2)}) collective-permute-start(bf16[512,768]{1,0:T(8,128)(2,1)S(1)} %fusion.2), channel_id=1, source_target_pairs={{0,1},{1,0},{2,3},{3,2},{4,5},{5,4},{6,7},{7,6},{8,9},{9,8},{10,11... | collective-permute-start | bytes 2359304 | tf_op jit(solution)/shard_map/ppermute | solution.py:363
  33.8 26.1 %copy-start.18 = (f32[768]{0:T(1024)S(1)}, f32[768]{0:T(1024)}, u32[]{:S(2)}) copy-start(f32[768]{0:T(1024)} %param.28) | copy-start | bytes 9220
  33.8 26.0 %copy-start.25 = (f32[12]{0:T(128)S(1)}, f32[12]{0:T(128)}, u32[]{:S(2)}) copy-start(f32[12]{0:T(128)} %param.27) | copy-start | bytes 148
  33.8 26.2 %copy-start.19 = (f32[768]{0:T(1024)S(1)}, f32[768]{0:T(1024)}, u32[]{:S(2)}) copy-start(f32[768]{0:T(1024)} %param.22) | copy-start | bytes 9220
  33.8 26.2 %copy-start.24 = (f32[256]{0:T(256)S(1)}, f32[256]{0:T(256)}, u32[]{:S(2)}) copy-start(f32[256]{0:T(256)} %param.24) | copy-start | bytes 3076
  33.8 26.2 %copy-start.26 = (f32[12]{0:T(128)S(1)}, f32[12]{0:T(128)}, u32[]{:S(2)}) copy-start(f32[12]{0:T(128)} %param.26) | copy-start | bytes 148
  33.8 26.2 %copy-start.27 = (f32[12]{0:T(128)S(1)}, f32[12]{0:T(128)}, u32[]{:S(2)}) copy-start(f32[12]{0:T(128)} %param.25) | copy-start | bytes 148
  33.8 27.4 %copy-start.17 = (f32[4,768]{1,0:T(4,128)S(1)}, f32[4,768]{1,0:T(4,128)}, u32[]{:S(2)}) copy-start(f32[4,768]{1,0:T(4,128)} %param.21) | copy-start | bytes 36868
  33.8 27.4 %copy-start.20 = (f32[4,256]{1,0:T(4,128)S(1)}, f32[4,256]{1,0:T(4,128)}, u32[]{:S(2)}) copy-start(f32[4,256]{1,0:T(4,128)} %param.23) | copy-start | bytes 12292
  58.3 19.9 %collective-permute-start.1 = (bf16[512,768]{1,0:T(8,128)(2,1)S(1)}, bf16[512,768]{1,0:T(8,128)(2,1)}, u32[]{:S(2)}, u32[]{:S(2)}) collective-permute-start(bf16[512,768]{1,0:T(8,128)(2,1)S(1)} %bitcast.125), channel_id=1, source_target_pairs={{0,1},{1,0},{2,3},{3,2},{4,5},{5,4},{6,7},{7,6},{8,9},{9,8},{10,11... | collective-permute-start | bytes 2359304 | tf_op jit(solution)/shard_map/ppermute | solution.py:363
  106.3 4.0 %collective-permute-start.2 = (f32[8,1024]{1,0:T(8,128)S(1)}, f32[8,1024]{1,0:T(8,128)S(1)}, u32[]{:S(2)}, u32[]{:S(2)}) collective-permute-start(f32[8,1024]{1,0:T(8,128)S(1)} %select_maximum_fusion), channel_id=1, source_target_pairs={{0,1},{1,0},{2,3},{3,2},{4,5},{5,4},{6,7},{7,6},{8,9},{9,8},{10,11... | collective-permute-start | bytes 98312 | tf_op jit(solution)/shard_map/ppermute | solution.py:363
  115.6 49.1 %collective-permute-start.3 = (bf16[512,768]{1,0:T(8,128)(2,1)S(1)}, bf16[512,768]{1,0:T(8,128)(2,1)}, u32[]{:S(2)}, u32[]{:S(2)}) collective-permute-start(bf16[512,768]{1,0:T(8,128)(2,1)S(1)} %constant_dynamic-slice_fusion.3), channel_id=1, source_target_pairs={{0,1},{1,0},{2,3},{3,2},{4,5},{5,4},{6,7},{7,6},{8,9},{9,8},{10,11... | collective-permute-start | bytes 2359304 | tf_op jit(solution)/shard_map/ppermute | solution.py:363
  117.3 47.3 %collective-permute-start.4 = (bf16[2,2,2,48,768]{4,3,0,1,2:T(8,128)(2,1)S(1)}, bf16[2,2,2,48,768]{4,3,0,1,2:T(8,128)(2,1)S(1)}, u32[]{:S(2)}, u32[]{:S(2)}) collective-permute-start(bf16[2,2,2,48,768]{4,3,0,1,2:T(8,128)(2,1)S(1)} %bitcast.131), channel_id=1, source_target_pairs={{0,4},{2,6},{4,0},{6,2},{8,12},{10,14},{12,8},{14,10},{16,20},{18,... | collective-permute-start | bytes 1769480 | tf_op jit(solution)/shard_map/ppermute | solution.py:363
  166.3 5.5 %collective-permute-start.19 = (bf16[2,2,48,768]{3,2,0,1:T(8,128)(2,1)S(1)}, bf16[2,2,48,768]{3,2,0,1:T(8,128)(2,1)S(1)}, u32[]{:S(2)}, u32[]{:S(2)}) collective-permute-start(bf16[2,2,48,768]{3,2,0,1:T(8,128)(2,1)S(1)} %dynamic-slice_bitcast_fusion.4), channel_id=1, source_target_pairs={{0,2},{2,0},{4,6},{6,4},{8,10},{10,8},{12,14},{14,12},{16,18},{18,... | collective-permute-start | bytes 884744 | tf_op jit(solution)/shard_map/ppermute | solution.py:363
  171.9 6.3 %collective-permute-start.20 = (bf16[2,48,768]{2,1,0:T(8,128)(2,1)S(1)}, bf16[2,48,768]{2,1,0:T(8,128)(2,1)S(1)}, u32[]{:S(2)}, u32[]{:S(2)}) collective-permute-start(bf16[2,48,768]{2,1,0:T(8,128)(2,1)S(1)} %dynamic-slice_bitcast_fusion.7), channel_id=1, source_target_pairs={{0,8},{2,10},{4,12},{6,14},{8,0},{10,2},{12,4},{14,6},{16,24},{18,... | collective-permute-start | bytes 442376 | tf_op jit(solution)/shard_map/ppermute | solution.py:363
  174.6 19.7 %collective-permute-start.5 = (bf16[512,768]{1,0:T(8,128)(2,1)S(1)}, bf16[512,768]{1,0:T(8,128)(2,1)S(1)}, u32[]{:S(2)}, u32[]{:S(2)}) collective-permute-start(bf16[512,768]{1,0:T(8,128)(2,1)S(1)} %constant_dynamic-slice_fusion), channel_id=1, source_target_pairs={{0,1},{1,0},{2,3},{3,2},{4,5},{5,4},{6,7},{7,6},{8,9},{9,8},{10,11... | collective-permute-start | bytes 2359304 | tf_op jit(solution)/shard_map/ppermute | solution.py:363
  175.7 9.8 %collective-permute-start.15 = (bf16[2,2,2,48,896]{4,3,2,1,0:T(8,128)(2,1)S(1)}, bf16[2,2,2,48,896]{4,3,2,1,0:T(8,128)(2,1)S(1)}, u32[]{:S(2)}, u32[]{:S(2)}) collective-permute-start(bf16[2,2,2,48,896]{4,3,2,1,0:T(8,128)(2,1)S(1)} %dynamic-slice_bitcast_fusion.1), channel_id=1, source_target_pairs={{0,2},{2,0},{4,6},{6,4},{8,10},{10,8},{12,14},{14,12},{16,18},{18,... | collective-permute-start | bytes 2064392 | tf_op jit(solution)/shard_map/ppermute | solution.py:363
  178.3 6.5 %collective-permute-start.21 = (bf16[48,768]{1,0:T(8,128)(2,1)S(1)}, bf16[48,768]{1,0:T(8,128)(2,1)S(1)}, u32[]{:S(2)}, u32[]{:S(2)}) collective-permute-start(bf16[48,768]{1,0:T(8,128)(2,1)S(1)} %dynamic-slice_bitcast_fusion.10), channel_id=1, source_target_pairs={{0,16},{2,18},{4,20},{6,22},{8,24},{10,26},{12,28},{14,30},{16,0},... | collective-permute-start | bytes 221192 | tf_op jit(solution)/shard_map/ppermute | solution.py:363
  180.1 15.4 %collective-permute-start.6 = (bf16[2,2,2,48,1024]{4,3,2,1,0:T(8,128)(2,1)S(1)}, bf16[2,2,2,48,1024]{4,3,2,1,0:T(8,128)(2,1)}, u32[]{:S(2)}, u32[]{:S(2)}) collective-permute-start(bf16[2,2,2,48,1024]{4,3,2,1,0:T(8,128)(2,1)S(1)} %dynamic-slice_bitcast_fusion), channel_id=1, source_target_pairs={{0,2},{2,0},{4,6},{6,4},{8,10},{10,8},{12,14},{14,12},{16,18},{18,... | collective-permute-start | bytes 2359304 | tf_op jit(solution)/shard_map/ppermute | solution.py:363
  186.7 28.3 %collective-permute-start.16 = (bf16[2,2,48,896]{3,2,1,0:T(8,128)(2,1)}, bf16[2,2,48,896]{3,2,1,0:T(8,128)(2,1)}, u32[]{:S(2)}, u32[]{:S(2)}) collective-permute-start(bf16[2,2,48,896]{3,2,1,0:T(8,128)(2,1)} %dynamic-slice_bitcast_fusion.3), channel_id=1, source_target_pairs={{0,4},{2,6},{4,0},{6,2},{8,12},{10,14},{12,8},{14,10},{16,20},{18,... | collective-permute-start | bytes 1032200 | tf_op jit(solution)/shard_map/ppermute | solution.py:363
  195.4 1.9 collective-permute-start.10
  197.4 3.9 %collective-permute-start.11 = (f32[56,128]{1,0:T(8,128)S(1)}, f32[56,128]{1,0:T(8,128)S(1)}, u32[]{:S(2)}, u32[]{:S(2)}) collective-permute-start(f32[56,128]{1,0:T(8,128)S(1)} %fusion.38), channel_id=1, source_target_pairs={{0,4},{2,6},{4,0},{6,2},{8,12},{10,14},{12,8},{14,10},{16,20},{18,... | collective-permute-start | bytes 86024 | tf_op jit(solution)/shard_map/ppermute | solution.py:363
  201.3 4.2 %collective-permute-start.12 = (f32[56,128]{1,0:T(8,128)S(1)}, f32[56,128]{1,0:T(8,128)S(1)}, u32[]{:S(2)}, u32[]{:S(2)}) collective-permute-start(f32[56,128]{1,0:T(8,128)S(1)} %fusion.43), channel_id=1, source_target_pairs={{0,8},{2,10},{4,12},{6,14},{8,0},{10,2},{12,4},{14,6},{16,24},{18,... | collective-permute-start | bytes 86024 | tf_op jit(solution)/shard_map/ppermute | solution.py:363
  202.8 16.2 %collective-permute-start.7 = (bf16[2,2,48,1024]{3,2,1,0:T(8,128)(2,1)}, bf16[2,2,48,1024]{3,2,1,0:T(8,128)(2,1)S(1)}, u32[]{:S(2)}, u32[]{:S(2)}) collective-permute-start(bf16[2,2,48,1024]{3,2,1,0:T(8,128)(2,1)} %dynamic-slice_bitcast_fusion.2), channel_id=1, source_target_pairs={{0,8},{2,10},{4,12},{6,14},{8,0},{10,2},{12,4},{14,6},{16,24},{18,... | collective-permute-start | bytes 1179656 | tf_op jit(solution)/shard_map/ppermute | solution.py:363
  205.5 7.0 %collective-permute-start.13 = (f32[56,128]{1,0:T(8,128)S(1)}, f32[56,128]{1,0:T(8,128)S(1)}, u32[]{:S(2)}, u32[]{:S(2)}) collective-permute-start(f32[56,128]{1,0:T(8,128)S(1)} %add.196), channel_id=1, source_target_pairs={{0,16},{2,18},{4,20},{6,22},{8,24},{10,26},{12,28},{14,30},{16,0},... | collective-permute-start | bytes 86024 | tf_op jit(solution)/shard_map/ppermute | solution.py:363
  216.2 7.3 %collective-permute-start.17 = (bf16[2,48,896]{2,1,0:T(8,128)(2,1)S(1)}, bf16[2,48,896]{2,1,0:T(8,128)(2,1)S(1)}, u32[]{:S(2)}, u32[]{:S(2)}) collective-permute-start(bf16[2,48,896]{2,1,0:T(8,128)(2,1)S(1)} %dynamic-slice_bitcast_fusion.6), channel_id=1, source_target_pairs={{0,8},{2,10},{4,12},{6,14},{8,0},{10,2},{12,4},{14,6},{16,24},{18,... | collective-permute-start | bytes 516104 | tf_op jit(solution)/shard_map/ppermute | solution.py:363
  219.2 12.2 %collective-permute-start.8 = (bf16[2,48,1024]{2,1,0:T(8,128)(2,1)S(1)}, bf16[2,48,1024]{2,1,0:T(8,128)(2,1)S(1)}, u32[]{:S(2)}, u32[]{:S(2)}) collective-permute-start(bf16[2,48,1024]{2,1,0:T(8,128)(2,1)S(1)} %dynamic-slice_bitcast_fusion.5), channel_id=1, source_target_pairs={{0,16},{2,18},{4,20},{6,22},{8,24},{10,26},{12,28},{14,30},{16,0},... | collective-permute-start | bytes 589832 | tf_op jit(solution)/shard_map/ppermute | solution.py:363
  223.6 9.3 %collective-permute-start.18 = (bf16[48,896]{1,0:T(8,128)(2,1)S(1)}, bf16[48,896]{1,0:T(8,128)(2,1)S(1)}, u32[]{:S(2)}, u32[]{:S(2)}) collective-permute-start(bf16[48,896]{1,0:T(8,128)(2,1)S(1)} %dynamic-slice_bitcast_fusion.9), channel_id=1, source_target_pairs={{0,16},{2,18},{4,20},{6,22},{8,24},{10,26},{12,28},{14,30},{16,0},... | collective-permute-start | bytes 258056 | tf_op jit(solution)/shard_map/ppermute | solution.py:363
  231.4 4.7 %collective-permute-start.9 = (bf16[48,1024]{1,0:T(8,128)(2,1)S(1)}, bf16[48,1024]{1,0:T(8,128)(2,1)S(1)}, u32[]{:S(2)}, u32[]{:S(2)}) collective-permute-start(bf16[48,1024]{1,0:T(8,128)(2,1)S(1)} %dynamic-slice_bitcast_fusion.8), channel_id=1, source_target_pairs={{0,4},{2,6},{4,0},{6,2},{8,12},{10,14},{12,8},{14,10},{16,20},{18,... | collective-permute-start | bytes 294920 | tf_op jit(solution)/shard_map/ppermute | solution.py:363
  236.2 4.2 %collective-permute-start.14 = (f32[112,128]{1,0:T(8,128)S(1)}, f32[112,128]{1,0:T(8,128)S(1)}, u32[]{:S(2)}, u32[]{:S(2)}) collective-permute-start(f32[112,128]{1,0:T(8,128)S(1)} %maximum_bitcast_fusion), channel_id=1, source_target_pairs={{0,1},{1,0},{2,3},{3,2},{4,5},{5,4},{6,7},{7,6},{8,9},{9,8},{10,11... | collective-permute-start | bytes 172040 | tf_op jit(solution)/shard_map/ppermute | solution.py:363
  (22 other events, 161.5 us)
Sparse Core Ops, SparseCore 0:
  10.8 47.4 all-gather.2
  60.5 36.6 all-gather.4
